TPU v7x, 32 devices: a whole 2x2x4 slice. The times are simulated.
32 devices in a mesh: dp: 8 (over z, x), blk: 4 (over y, core).
Axes of the slice: x: 2, y: 2, z: 4, core: 2. Of those that a mesh axis runs over, the one named last changes fastest.
Arguments:
- layer_input: bfloat16 [16, 1024, 768], P('dp', 'blk'), may hold values from -6 to 6
- doc_lengths: int32 [16, 8], P('dp'), may hold values from 0 to 1024, as said below
- w_qkv: bfloat16 [768, 2304], replicated, may hold values from -0.21875 to 0.21875
- b_query: float32 [768], replicated, may hold values from -3 to 3
- b_value: float32 [768], replicated, may hold values from -0.3 to 0.3
- w_out: bfloat16 [768, 768], replicated, may hold values from -0.875 to 0.875
- b_out: float32 [768], replicated, may hold values from -3 to 3
- w_fc: bfloat16 [768, 3072], replicated, may hold values from -0.21875 to 0.21875
- b_fc: float32 [3072], replicated, may hold values from -3 to 3
- w_proj: bfloat16 [3072, 768], replicated, may hold values from -0.109375 to 0.109375
- b_proj: float32 [768], replicated, may hold values from -3 to 3
- gain_one: float32 [768], replicated, may hold values from 0.1 to 1.9
- shift_one: float32 [768], replicated, may hold values from -3 to 3
- gain_two: float32 [768], replicated, may hold values from 0.1 to 1.9
- shift_two: float32 [768], replicated, may hold values from -3 to 3
- d_out: bfloat16 [16, 1024, 768], P('dp', 'blk'), may hold values from -6 to 6
Outputs:
- layer_output: bfloat16 [16, 1024, 768], P('dp', 'blk')
- grad_input: float32 [16, 1024, 768], P('dp', 'blk')
- grad_w_qkv: float32 [768, 2304], P('dp', 'blk')
- grad_b_query: float32 [768], P('dp')
- grad_b_value: float32 [768], P('dp')
- grad_w_out: float32 [768, 768], P('dp', 'blk')
- grad_b_out: float32 [768], P('dp')
- grad_w_fc: float32 [768, 3072], P('dp', 'blk')
- grad_b_fc: float32 [3072], P('dp')
- grad_w_proj: float32 [3072, 768], P('dp', 'blk')
- grad_b_proj: float32 [768], P('dp')
- grad_gain_one: float32 [768], P('dp')
- grad_shift_one: float32 [768], P('dp')
- grad_gain_two: float32 [768], P('dp')
- grad_shift_two: float32 [768], P('dp')
Inputs may be any that keep to these rules, and one draw needn't show every extreme that they name: `doc_lengths`: entry j of a row is the length of document j of that row (0 allowed); the entries of a row sum to 1024. Among the 2 rows of each index of dp, one row holds a single document of 1024 positions.
All inputs are finite; a program needn't handle non-finite values.
Results may differ from a plain program's by a relative error of at most 0.014.
Values may be sent and summed in bfloat16 or wider, within the bound.
A program may use at most 128 MiB of HBM per device.

v0:
```python
import jax
import jax.numpy as jnp
from jax import lax
from jax.sharding import PartitionSpec as P

HEADS = 12
HEAD = 64


ln_epsilon = 1e-05
gelu_factor = 0.7978845608028654
big_negative = -1e30


def shifted(shard, axis, by):
    size = lax.axis_size(axis)
    pairs = [(i, i + by) for i in range(size) if 0 <= i + by < size]
    return lax.ppermute(shard, axis, pairs)


def layer_stats(inputs):
    centre = jnp.mean(inputs, axis=-1, keepdims=True)
    centered = inputs - centre
    inverse = lax.rsqrt(jnp.mean(centered * centered, axis=-1, keepdims=True) + ln_epsilon)
    return (centered * inverse, inverse)


def norm_back(grad_norm, normed, inverse):
    first = jnp.mean(grad_norm, axis=-1, keepdims=True)
    second = jnp.mean(grad_norm * normed, axis=-1, keepdims=True)
    return inverse * (grad_norm - first - normed * second)


def gelu_tanh(inputs):
    return (
        0.5
        * inputs
        * (1.0 + jnp.tanh(gelu_factor * (inputs + 0.044715 * inputs * inputs * inputs)))
    )


def gelu_slope(inputs):
    inner = jnp.tanh(gelu_factor * (inputs + 0.044715 * inputs * inputs * inputs))
    return 0.5 * (1.0 + inner) + 0.5 * inputs * (1.0 - inner * inner) * gelu_factor * (
        1.0 + 3.0 * 0.044715 * inputs * inputs
    )


def doc_index(doc_ends, positions):
    return jnp.sum((doc_ends[:, None, :] <= positions[None, :, None]).astype(jnp.int32), axis=-1)


def attend_block(running, query, key_heads, value_heads, allowed, softmax_scale):
    run_max, run_sum, run_acc = running
    scores = (
        jnp.einsum("rqhd,rkhd->rhqk", query, key_heads, preferred_element_type=jnp.float32)
        * softmax_scale
    )
    scores = jnp.where(allowed[:, None], scores, big_negative)
    new_max = jnp.maximum(run_max, jnp.max(scores, axis=-1))
    factor = jnp.exp(run_max - new_max)
    weights = jnp.exp(scores - new_max[..., None])
    run_sum = run_sum * factor + jnp.sum(weights, axis=-1)
    update = jnp.einsum(
        "rhqk,rkhd->rhqd", weights, value_heads.astype(jnp.float32), precision=lax.Precision.HIGHEST
    )
    run_acc = run_acc * factor[..., None] + update
    return (new_max, run_sum, run_acc)


def attend_back(
    query,
    key_heads,
    value_heads,
    allowed,
    log_total,
    row_delta,
    grad_heads,
    grad_heads_wide,
    softmax_scale,
):
    scores = (
        jnp.einsum("rqhd,rkhd->rhqk", query, key_heads, preferred_element_type=jnp.float32)
        * softmax_scale
    )
    scores = jnp.where(allowed[:, None], scores, big_negative)
    attention = jnp.exp(scores - log_total[..., None])
    grad_attention = jnp.einsum(
        "rqhd,rkhd->rhqk", grad_heads, value_heads, preferred_element_type=jnp.float32
    )
    grad_scores = (attention * (grad_attention - row_delta[..., None])).astype(jnp.bfloat16)
    part_query = (
        jnp.einsum("rhqk,rkhd->rqhd", grad_scores, key_heads, preferred_element_type=jnp.float32)
        * softmax_scale
    )
    part_keys = (
        jnp.einsum("rhqk,rqhd->rkhd", grad_scores, query, preferred_element_type=jnp.float32)
        * softmax_scale
    )
    part_values = jnp.einsum(
        "rhqk,rqhd->rkhd", attention, grad_heads_wide, precision=lax.Precision.HIGHEST
    )
    return (part_query, part_keys, part_values)


def body(
    layer_input,
    doc_lengths,
    w_qkv,
    b_query,
    b_value,
    w_out,
    b_out,
    w_fc,
    b_fc,
    w_proj,
    b_proj,
    gain_one,
    shift_one,
    gain_two,
    shift_two,
    d_out,
):
    row_count, span_len, model_width = layer_input.shape
    blocks = lax.axis_size("blk")
    my_index = lax.axis_index("blk")
    softmax_scale = HEAD ** (-0.5)
    tokens = row_count * span_len
    inputs = layer_input.reshape(tokens, model_width).astype(jnp.float32)
    normed_one, inverse_one = layer_stats(inputs)
    attn_in = (normed_one * gain_one + shift_one).astype(jnp.bfloat16)
    projected = jnp.dot(attn_in, w_qkv, preferred_element_type=jnp.float32)
    query = (
        (projected[:, :model_width] + b_query)
        .astype(jnp.bfloat16)
        .reshape(row_count, span_len, HEADS, HEAD)
    )
    key_heads = (
        projected[:, model_width : 2 * model_width]
        .astype(jnp.bfloat16)
        .reshape(row_count, span_len, HEADS, HEAD)
    )
    value_heads = (
        (projected[:, 2 * model_width :] + b_value)
        .astype(jnp.bfloat16)
        .reshape(row_count, span_len, HEADS, HEAD)
    )
    doc_ends = jnp.cumsum(doc_lengths, axis=1)
    local_pos = jnp.arange(span_len, dtype=jnp.int32)
    query_pos = my_index * span_len + local_pos
    query_doc = doc_index(doc_ends, query_pos)

    def forward_step(running, offset, current, allowed):

        def active_step(state):
            return attend_block(state, query, current[0], current[1], allowed, softmax_scale)

        if offset == 0:
            return active_step(running)
        return lax.cond(my_index >= offset, active_step, lambda state: state, running)

    key_value = jnp.stack([key_heads, value_heads])
    running = (
        jnp.full((row_count, HEADS, span_len), big_negative, jnp.float32),
        jnp.zeros((row_count, HEADS, span_len), jnp.float32),
        jnp.zeros((row_count, HEADS, span_len, HEAD), jnp.float32),
    )
    stored = []
    current = key_value
    for offset in range(blocks):
        if offset > 0:
            current = shifted(current, "blk", 1)
        source = my_index - offset
        key_pos = source * span_len + local_pos
        key_doc = doc_index(doc_ends, key_pos)
        same_doc = query_doc[:, :, None] == key_doc[:, None, :]
        causal = key_pos[None, None, :] <= query_pos[None, :, None]
        allowed = same_doc & causal & (source >= 0)
        stored.append((current, allowed))
        running = forward_step(running, offset, current, allowed)
    run_max, run_sum, run_acc = running
    attn_full = run_acc / run_sum[..., None]
    log_total = run_max + jnp.log(run_sum)
    mixed_full = attn_full.transpose(0, 2, 1, 3).reshape(tokens, model_width)
    mixed_low = mixed_full.astype(jnp.bfloat16)
    residual = inputs + jnp.dot(mixed_low, w_out, preferred_element_type=jnp.float32) + b_out
    normed_two, inverse_two = layer_stats(residual)
    mlp_in = (normed_two * gain_two + shift_two).astype(jnp.bfloat16)
    hidden_pre = jnp.dot(mlp_in, w_fc, preferred_element_type=jnp.float32) + b_fc
    hidden_low = gelu_tanh(hidden_pre).astype(jnp.bfloat16)
    output = residual + jnp.dot(hidden_low, w_proj, preferred_element_type=jnp.float32) + b_proj
    result = output.astype(jnp.bfloat16).reshape(row_count, span_len, model_width)
    grad_top = d_out.reshape(tokens, model_width)
    grad_top_wide = grad_top.astype(jnp.float32)
    grad_wproj = jnp.einsum("tf,td->fd", hidden_low, grad_top, preferred_element_type=jnp.float32)
    grad_bproj = jnp.sum(grad_top_wide, axis=0)
    grad_hidden = jnp.einsum("td,fd->tf", grad_top, w_proj, preferred_element_type=jnp.float32)
    grad_pre = (grad_hidden * gelu_slope(hidden_pre)).astype(jnp.bfloat16)
    grad_wfc = jnp.einsum("td,tf->df", mlp_in, grad_pre, preferred_element_type=jnp.float32)
    grad_bfc = jnp.sum(grad_pre.astype(jnp.float32), axis=0)
    grad_mlp_in = jnp.einsum("tf,df->td", grad_pre, w_fc, preferred_element_type=jnp.float32)
    grad_gtwo = jnp.sum(grad_mlp_in * normed_two, axis=0)
    grad_stwo = jnp.sum(grad_mlp_in, axis=0)
    grad_residual = grad_top_wide + norm_back(grad_mlp_in * gain_two, normed_two, inverse_two)
    grad_branch = grad_residual.astype(jnp.bfloat16)
    grad_wout = jnp.einsum("td,te->de", mixed_low, grad_branch, preferred_element_type=jnp.float32)
    grad_bout = jnp.sum(grad_branch.astype(jnp.float32), axis=0)
    grad_mixed = jnp.einsum(
        "te,de->td", grad_branch, w_out, preferred_element_type=jnp.float32
    ).astype(jnp.bfloat16)
    grad_heads = grad_mixed.reshape(row_count, span_len, HEADS, HEAD)
    grad_heads_wide = grad_heads.astype(jnp.float32)
    row_delta = jnp.sum(grad_heads_wide.transpose(0, 2, 1, 3) * attn_full, axis=-1)

    def backward_step(offset, current, allowed):

        def active_back(unused):
            return attend_back(
                query,
                current[0],
                current[1],
                allowed,
                log_total,
                row_delta,
                grad_heads,
                grad_heads_wide,
                softmax_scale,
            )

        def skipped_back(unused):
            empty = jnp.zeros((row_count, span_len, HEADS, HEAD), jnp.float32)
            return (empty, empty, empty)

        if offset == 0:
            return active_back(None)
        return lax.cond(my_index >= offset, active_back, skipped_back, None)

    grad_query = jnp.zeros((row_count, span_len, HEADS, HEAD), jnp.float32)
    carried = None
    for offset in reversed(range(blocks)):
        current, allowed = stored[offset]
        part_query, part_keys, part_values = backward_step(offset, current, allowed)
        grad_query = grad_query + part_query
        local_term = jnp.stack([part_keys, part_values])
        if carried is None:
            carried = local_term
        else:
            carried = (
                shifted(carried.astype(jnp.bfloat16), "blk", -1).astype(carried.dtype) + local_term
            )
    grad_query_low = grad_query.astype(jnp.bfloat16).reshape(tokens, model_width)
    grad_keys_low = carried[0].astype(jnp.bfloat16).reshape(tokens, model_width)
    grad_values_low = carried[1].astype(jnp.bfloat16).reshape(tokens, model_width)
    grad_bquery = jnp.sum(grad_query_low.astype(jnp.float32), axis=0)
    grad_bvalue = jnp.sum(grad_values_low.astype(jnp.float32), axis=0)
    grad_joint = jnp.concatenate([grad_query_low, grad_keys_low, grad_values_low], axis=1)
    grad_wqkv = jnp.einsum("td,te->de", attn_in, grad_joint, preferred_element_type=jnp.float32)
    grad_attn_in = jnp.einsum("te,de->td", grad_joint, w_qkv, preferred_element_type=jnp.float32)
    grad_gone = jnp.sum(grad_attn_in * normed_one, axis=0)
    grad_sone = jnp.sum(grad_attn_in, axis=0)
    grad_inputs = grad_residual + norm_back(grad_attn_in * gain_one, normed_one, inverse_one)
    parts = (
        lax.psum_scatter(grad_wqkv, "dp", scatter_dimension=0, tiled=True),
        lax.psum_scatter(grad_wout, "dp", scatter_dimension=0, tiled=True),
        lax.psum_scatter(grad_wfc, "dp", scatter_dimension=0, tiled=True),
        lax.psum_scatter(grad_wproj, "dp", scatter_dimension=0, tiled=True),
        lax.psum_scatter(grad_bquery, "dp", scatter_dimension=0, tiled=True),
        lax.psum_scatter(grad_bvalue, "dp", scatter_dimension=0, tiled=True),
        lax.psum_scatter(grad_bout, "dp", scatter_dimension=0, tiled=True),
        lax.psum_scatter(grad_bfc, "dp", scatter_dimension=0, tiled=True),
        lax.psum_scatter(grad_bproj, "dp", scatter_dimension=0, tiled=True),
        lax.psum_scatter(grad_gone, "dp", scatter_dimension=0, tiled=True),
        lax.psum_scatter(grad_sone, "dp", scatter_dimension=0, tiled=True),
        lax.psum_scatter(grad_gtwo, "dp", scatter_dimension=0, tiled=True),
        lax.psum_scatter(grad_stwo, "dp", scatter_dimension=0, tiled=True),
    )
    matrices = (
        lax.psum_scatter(
            parts[0].astype(jnp.bfloat16), "blk", scatter_dimension=1, tiled=True
        ).astype(jnp.float32),
        lax.psum_scatter(
            parts[1].astype(jnp.bfloat16), "blk", scatter_dimension=1, tiled=True
        ).astype(jnp.float32),
        lax.psum_scatter(
            parts[2].astype(jnp.bfloat16), "blk", scatter_dimension=1, tiled=True
        ).astype(jnp.float32),
        lax.psum_scatter(
            parts[3].astype(jnp.bfloat16), "blk", scatter_dimension=1, tiled=True
        ).astype(jnp.float32),
    )
    vectors = lax.psum(
        (
            parts[4],
            parts[5],
            parts[6],
            parts[7],
            parts[8],
            parts[9],
            parts[10],
            parts[11],
            parts[12],
        ),
        "blk",
    )
    return (
        result,
        grad_inputs.reshape(row_count, span_len, model_width),
        matrices[0],
        vectors[0],
        vectors[1],
        matrices[1],
        vectors[2],
        matrices[2],
        vectors[3],
        matrices[3],
        vectors[4],
        vectors[5],
        vectors[6],
        vectors[7],
        vectors[8],
    )


def solution(mesh):
    in_specs = (
        P("dp", "blk", None),
        P("dp", None),
        P(),
        P(),
        P(),
        P(),
        P(),
        P(),
        P(),
        P(),
        P(),
        P(),
        P(),
        P(),
        P(),
        P("dp", "blk", None),
    )
    out_specs = (
        P("dp", "blk", None),
        P("dp", "blk", None),
        P("dp", "blk"),
        P("dp"),
        P("dp"),
        P("dp", "blk"),
        P("dp"),
        P("dp", "blk"),
        P("dp"),
        P("dp", "blk"),
        P("dp"),
        P("dp"),
        P("dp"),
        P("dp"),
        P("dp"),
    )
    return jax.shard_map(body, mesh=mesh, in_specs=in_specs, out_specs=out_specs, check_vma=False)
```

profile of v0, /device:TPU:0, one launch (start us, length us, event | category | flops | bytes accessed | tf_op | source)
XLA Modules:
  0.0 852.3 jit_solution(5174141732290402195)
XLA Ops:
  12.4 2.0 fusion.149
  14.4 2.1 copy-done.24
  17.5 2.3 copy.173
  19.8 3.3 fusion.103
  23.1 2.3 copy.176
  25.4 2.9 stack_reshape.7
  28.3 2.9 stack_reshape.6
  31.2 3.7 pad_maximum_fusion
  34.9 3.5 collective-permute-start
  38.4 2.0 collective-permute-done
  40.5 20.1 %collective-permute-start.1 = (bf16[2,2,256,12,64]{2,1,4,3,0:T(2,128)(2,1)}, bf16[2,2,256,12,64]{2,1,4,3,0:T(2,128)(2,1)}, u32[]{:S(2)}, u32[]{:S(2)}) collective-permute-start(bf16[2,2,256,12,64]{2,1,4,3,0:T(2,128)(2,1)} %collective-permute-done), channel_id=1, source_target_pairs={{0,1},{1,2},{2,3},{4,5},{5,6},{6,7},{8,9},{9,10},{10,11},{12,13},{... | collective-permute-start | bytes 4718600 | tf_op jit(solution)/shard_map/ppermute | solution.py:18
  60.6 2.9 squeeze_stack_reshape.8
  65.4 1.8 copy.171
  67.1 2.3 copy.172
  69.4 2.9 reshape.307
  72.3 10.2 %collective-permute-start.2 = (bf16[2,2,256,12,64]{2,1,4,3,0:T(2,128)(2,1)}, bf16[2,2,256,12,64]{2,1,4,3,0:T(2,128)(2,1)}, u32[]{:S(2)}, u32[]{:S(2)}) collective-permute-start(bf16[2,2,256,12,64]{2,1,4,3,0:T(2,128)(2,1)} %collective-permute-done.1), channel_id=1, source_target_pairs={{0,1},{1,2},{2,3},{4,5},{5,6},{6,7},{8,9},{9,10},{10,11},{12,13},{... | collective-permute-start | bytes 4718600 | tf_op jit(solution)/shard_map/ppermute | solution.py:18
  82.5 5.9 fusion.92
  88.3 2.9 squeeze_stack_reshape.9
  92.6 4.3 fusion.90
  97.5 6.0 fusion.123
  104.0 5.5 conditional.7
  109.5 8.7 %conditional.8 = (f32[2,12,256]{2,1,0:T(8,128)}, f32[2,12,256,64]{2,3,1,0:T(8,128)}, f32[2,12,256]{2,1,0:T(8,128)}) conditional(s32[]{:T(128)} %convert_element_type.169, (f32[2,12,256]{2,1,0:T(8,128)}, f32[2,12,256]{2,1,0:T(8,128)}, f32[2,12,256,64]{2,3,1,0:T(8,128)}) %get-tuple-element.560, (pred[2,256,256]{2,1,0:T(8,128)(4,1)}, ...), branch_computations={%region_17.18_spmd.clone, %region_18.21_spmd.clone} | conditional | flops 1425813504 | bytes 45039808 | solution.py:160
  119.1 4.2 fusion.147
  124.9 1.8 copy-done.64
  126.7 2.7 fusion.144
  129.5 7.2 convert_reduce_fusion
  136.8 3.6 multiply_reduce_fusion
  142.7 1.7 convolution_convert_fusion
  144.5 2.4 copy.192
  146.8 2.9 reshape.310
  149.7 3.1 convert_element_type.190
  154.2 3.0 fusion.106
  161.2 13.6 %collective-permute-done.3 = bf16[2,2,256,12,64]{2,4,3,1,0:T(8,128)(2,1)} collective-permute-done((bf16[2,2,256,12,64]{2,4,3,1,0:T(8,128)(2,1)}, bf16[2,2,256,12,64]{2,4,3,1,0:T(8,128)(2,1)}, u32[]{:S(2)}, u32[]{:S(2)}) %collective-permute-start.3) | collective-permute-done | bytes 1572896 | tf_op jit(solution)/shard_map/ppermute | solution.py:18
  174.8 3.3 fusion.93
  179.4 2.2 fusion.134
  183.7 5.9 multiply_convert_fusion.4
  189.6 14.6 %collective-permute-done.4 = bf16[2,2,256,12,64]{2,4,3,1,0:T(8,128)(2,1)} collective-permute-done((bf16[2,2,256,12,64]{2,4,3,1,0:T(8,128)(2,1)}, bf16[2,2,256,12,64]{2,4,3,1,0:T(8,128)(2,1)}, u32[]{:S(2)}, u32[]{:S(2)}) %collective-permute-start.4) | collective-permute-done | bytes 1572896 | tf_op jit(solution)/shard_map/ppermute | solution.py:18
  204.2 2.0 fusion.94
  212.1 5.2 fusion.122
  217.2 17.2 %collective-permute-done.5 = bf16[2,2,256,12,64]{2,4,3,1,0:T(8,128)(2,1)S(1)} collective-permute-done((bf16[2,2,256,12,64]{2,4,3,1,0:T(8,128)(2,1)S(1)}, bf16[2,2,256,12,64]{2,4,3,1,0:T(8,128)(2,1)S(1)}, u32[]{:S(2)}, u32[]{:S(2)}) %collective-permute-start.5) | collective-permute-done | bytes 1572896 | tf_op jit(solution)/shard_map/ppermute | solution.py:18
  239.0 5.0 fusion.150
  244.4 10.5 %fusion.145 = f32[3072,768]{1,0:T(8,128)} fusion(bf16[512,768]{1,0:T(8,128)(2,1)} %bitcast.208, f32[512,3072]{1,0:T(8,128)} %copy-done.69, f32[3072]{0:T(1024)} %param.36), kind=kOutput, calls=%fused_computation.246 | convolution fusion | flops 2431647744 | bytes 16527360 | tf_op jit(solution)/shard_map/tf,td->fd/dot_general | solution.py:195
  255.1 9.0 %fusion.143 = f32[768,3072]{1,0:T(8,128)} fusion(bf16[512,3072]{1,0:T(8,128)(2,1)} %copy-done.70, f32[512,768]{1,0:T(8,128)} %copy-done.16, f32[768]{0:T(1024)} %param.42, f32[768]{0:T(1024)} %param.41, f32[512]{0:T(512)} %copy-done.59, f32[512]{0:T(512)} %copy-done.56), kind=kOutput, calls=%fused_computation.244 | convolution fusion | flops 2417885184 | bytes 14166016 | tf_op jit(solution)/shard_map/td,tf->df/dot_general | solution.py:199
  264.2 19.0 %reduce-scatter.17.cloned.1.call-done = f32[96,768]{1,0:T(8,128)} async-done(((f32[768,768]{1,0:T(8,128)}), f32[96,768]{1,0:T(8,128)}) %reduce-scatter.17.cloned.1.call-update) | async-done | bytes 294928 | tf_op jit(solution)/shard_map/reduce_scatter | solution.py:264
  284.8 1.7 copy.232
  286.6 128.3 %reduce-scatter.15.cloned.1.call-done = f32[96,2304]{1,0:T(8,128)} async-done(((f32[768,2304]{1,0:T(8,128)}), f32[96,2304]{1,0:T(8,128)}) %reduce-scatter.15.cloned.1.call-update) | async-done | bytes 884752 | tf_op jit(solution)/shard_map/reduce_scatter | solution.py:263
  414.9 2.0 convert_element_type.201
  416.9 2.1 copy.230
  419.0 162.3 %reduce-scatter.23.cloned.1.call-done = f32[384,768]{1,0:T(8,128)} async-done(((f32[3072,768]{1,0:T(8,128)}), f32[384,768]{1,0:T(8,128)}) %reduce-scatter.23.cloned.1.call-update) | async-done | bytes 1179664 | tf_op jit(solution)/shard_map/reduce_scatter | solution.py:266
  581.3 2.1 convert_element_type.211
  583.5 2.2 copy.234
  585.9 1.9 convert_reduce_fusion.2
  590.9 10.0 %add_convert_fusion = bf16[512,768]{1,0:T(8,128)(2,1)} fusion(f32[512,768]{1,0:T(8,128)} %copy-done.16, bf16[3072,768]{1,0:T(8,128)(2,1)} %param.37, f32[768]{0:T(1024)} %param.38, f32[512,3072]{1,0:T(8,128)} %copy-done.69, f32[3072]{0:T(1024)} %param.36), kind=kOutput, calls=%fused_computation.186 | convolution fusion | flops 2432827392 | bytes 13384704 | tf_op jit(solution)/shard_map/dot_general | solution.py:191
  601.6 146.0 %reduce-scatter.19.cloned.1.call-done = f32[96,3072]{1,0:T(8,128)} async-done(((f32[768,3072]{1,0:T(8,128)}), f32[96,3072]{1,0:T(8,128)}) %reduce-scatter.19.cloned.1.call-update) | async-done | bytes 1179664 | tf_op jit(solution)/shard_map/reduce_scatter | solution.py:265
  747.6 2.2 convert_element_type.208
  749.9 6.0 fusion.120
  755.9 36.8 %all-reduce.9 = (f32[768]{0:T(1024)}, f32[768]{0:T(1024)}, f32[768]{0:T(1024)}, f32[3072]{0:T(1024)}, f32[768]{0:T(1024)}, /*index=5*/f32[768]{0:T(1024)}, f32[768]{0:T(1024)}, f32[768]{0:T(1024)}, f32[768]{0:T(1024)}) all-reduce(f32[768]{0:T(1024)} %reduce_sum.257, ...), channel_id=4, replica_groups=mesh['dp'=8,'blk'=4] {'dp'}, use_global_device_ids=true, to_apply=%region_37.38.clone | all-reduce | flops 9216 | bytes 73728
  803.5 6.4 all-reduce.10
  811.3 3.9 fusion.119
  818.2 1.7 copy.231
  821.5 1.7 copy.235
  823.2 1.8 copy.221
  824.9 18.7 %reduce-scatter.21.cloned.1.call-done = bf16[96,768]{1,0:T(8,128)(2,1)} async-done(((bf16[96,3072]{1,0:T(8,128)(2,1)}), bf16[96,768]{1,0:T(8,128)(2,1)}) %reduce-scatter.21.cloned.1.call-update) | async-done | bytes 147472 | tf_op jit(solution)/shard_map/reduce_scatter | solution.py:284
  843.6 1.6 convert_element_type.209
  (206 shorter events, 57.2 us)
Async XLA Ops:
  7.2 5.2 copy-start
  7.2 276.0 %reduce-scatter.17.cloned.1.call-start = ((), (), s32[]{:S(2)}) async-start(), calls=%async_computation.9 | async-start | bytes 2654208 | tf_op jit(solution)/shard_map/reduce_scatter | solution.py:264
  12.4 2.0 copy-start.25
  14.4 2.1 copy-start.24
  16.5 3.3 copy-start.60
  16.5 3.3 copy-start.61
  28.3 35.2 %copy-start.63 = (s32[2,8]{1,0:T(2,128)S(1)}, s32[2,8]{1,0:T(2,128)}, u32[]{:S(2)}) copy-start(s32[2,8]{1,0:T(2,128)} %param.29) | copy-start | bytes 196
  34.9 5.5 collective-permute-start
  40.5 31.9 %collective-permute-start.1 = (bf16[2,2,256,12,64]{2,1,4,3,0:T(2,128)(2,1)}, bf16[2,2,256,12,64]{2,1,4,3,0:T(2,128)(2,1)}, u32[]{:S(2)}, u32[]{:S(2)}) collective-permute-start(bf16[2,2,256,12,64]{2,1,4,3,0:T(2,128)(2,1)} %collective-permute-done), channel_id=1, source_target_pairs={{0,1},{1,2},{2,3},{4,5},{5,6},{6,7},{8,9},{9,10},{10,11},{12,13},{... | collective-permute-start | bytes 4718600 | tf_op jit(solution)/shard_map/ppermute | solution.py:18
  72.3 37.2 %collective-permute-start.2 = (bf16[2,2,256,12,64]{2,1,4,3,0:T(2,128)(2,1)}, bf16[2,2,256,12,64]{2,1,4,3,0:T(2,128)(2,1)}, u32[]{:S(2)}, u32[]{:S(2)}) collective-permute-start(bf16[2,2,256,12,64]{2,1,4,3,0:T(2,128)(2,1)} %collective-permute-done.1), channel_id=1, source_target_pairs={{0,1},{1,2},{2,3},{4,5},{5,6},{6,7},{8,9},{9,10},{10,11},{12,13},{... | collective-permute-start | bytes 4718600 | tf_op jit(solution)/shard_map/ppermute | solution.py:18
  92.6 4.3 copy-start.51
  92.6 4.9 copy-start.15
  92.6 4.9 copy-start.43
  118.2 5.3 copy-start.10
  118.2 5.3 copy-start.65
  118.2 5.3 copy-start.67
  119.1 5.7 copy-start.68
  123.5 1.4 copy-start.27
  123.5 1.3 copy-start.62
  123.5 3.2 copy-start.64
  123.6 5.9 slice-start.2
  124.5 15.8 %copy-start.16 = (f32[512,768]{1,0:T(8,128)}, f32[512,768]{1,0:T(8,128)S(1)}, u32[]{:S(2)}) copy-start(f32[512,768]{1,0:T(8,128)S(1)} %get-tuple-element.514) | copy-start | bytes 4718596
  124.5 15.8 %copy-start.56 = (f32[512]{0:T(512)}, f32[512]{0:T(512)S(1)}, u32[]{:S(2)}) copy-start(f32[512]{0:T(512)S(1)} %broadcast_multiply_fusion.4) | copy-start | bytes 6148
  126.7 13.6 %copy-start.59 = (f32[512]{0:T(512)}, f32[512]{0:T(512)S(1)}, u32[]{:S(2)}) copy-start(f32[512]{0:T(512)S(1)} %add_rsqrt_fusion) | copy-start | bytes 6148
  126.7 2.8 copy-start.29
  126.7 2.8 slice-start.3
  126.7 2.8 copy-start.66
  129.5 7.3 copy-start.69
  136.8 3.6 copy-start.70
  149.7 7.6 copy-start.1
  149.7 7.6 copy-start.11
  149.7 7.6 copy-start.47
  157.8 2.8 copy-start.17
  157.8 2.8 copy-start.2
  157.8 2.8 copy-start.12
  157.8 2.8 copy-start.46
  159.2 15.6 %collective-permute-start.3 = (bf16[2,2,256,12,64]{2,4,3,1,0:T(8,128)(2,1)}, bf16[2,2,256,12,64]{2,4,3,1,0:T(8,128)(2,1)}, u32[]{:S(2)}, u32[]{:S(2)}) collective-permute-start(bf16[2,2,256,12,64]{2,4,3,1,0:T(8,128)(2,1)} %pad_maximum_fusion.1), channel_id=1, source_target_pairs={{1,0},{2,1},{3,2},{5,4},{6,5},{7,6},{9,8},{10,9},{11,10},{13,12},{... | collective-permute-start | bytes 4718600 | tf_op jit(solution)/shard_map/ppermute | solution.py:18
  161.2 16.9 %copy-start.19 = (f32[2,256,12,64]{1,3,2,0:T(8,128)}, f32[2,256,12,64]{1,3,2,0:T(8,128)S(1)}, u32[]{:S(2)}) copy-start(f32[2,256,12,64]{1,3,2,0:T(8,128)S(1)} %get-tuple-element.198) | copy-start | bytes 4718596
  174.8 4.6 copy-start.9
  174.8 4.6 copy-start.28
  178.1 26.1 %collective-permute-start.4 = (bf16[2,2,256,12,64]{2,4,3,1,0:T(8,128)(2,1)}, bf16[2,2,256,12,64]{2,4,3,1,0:T(8,128)(2,1)}, u32[]{:S(2)}, u32[]{:S(2)}) collective-permute-start(bf16[2,2,256,12,64]{2,4,3,1,0:T(8,128)(2,1)} %fusion.93), channel_id=1, source_target_pairs={{1,0},{2,1},{3,2},{5,4},{6,5},{7,6},{9,8},{10,9},{11,10},{13,12},{... | collective-permute-start | bytes 4718600 | tf_op jit(solution)/shard_map/ppermute | solution.py:18
  181.6 233.3 %reduce-scatter.15.cloned.1.call-start = ((), (), s32[]{:S(2)}) async-start(), calls=%async_computation.8 | async-start | bytes 7962624 | tf_op jit(solution)/shard_map/reduce_scatter | solution.py:263
  183.7 5.9 copy-start.21
  204.2 3.6 copy-start.30
  206.2 2.2 copy-start.18
  206.3 2.2 copy-start.20
  206.3 2.3 copy-start.22
  206.3 28.2 %collective-permute-start.5 = (bf16[2,2,256,12,64]{2,4,3,1,0:T(8,128)(2,1)S(1)}, bf16[2,2,256,12,64]{2,4,3,1,0:T(8,128)(2,1)S(1)}, u32[]{:S(2)}, u32[]{:S(2)}) collective-permute-start(bf16[2,2,256,12,64]{2,4,3,1,0:T(8,128)(2,1)S(1)} %fusion.94), channel_id=1, source_target_pairs={{1,0},{2,1},{3,2},{5,4},{6,5},{7,6},{9,8},{10,9},{11,10},{13,12},{... | collective-permute-start | bytes 4718600 | tf_op jit(solution)/shard_map/ppermute | solution.py:18
  208.6 2.8 slice-start
  209.0 2.8 slice-start.1
  210.0 2.1 copy-start.13
  210.0 2.1 copy-start.44
  236.4 2.6 copy-start.26
  237.5 1.5 copy-start.23
  244.0 337.3 %reduce-scatter.23.cloned.1.call-start = ((), (), s32[]{:S(2)}) async-start(), calls=%async_computation.12 | async-start | bytes 10616832 | tf_op jit(solution)/shard_map/reduce_scatter | solution.py:266
  255.0 492.6 %reduce-scatter.19.cloned.1.call-start = ((), (), s32[]{:S(2)}) async-start(), calls=%async_computation.10 | async-start | bytes 10616832 | tf_op jit(solution)/shard_map/reduce_scatter | solution.py:265
  264.1 551.1 %reduce-scatter.27.cloned.1.call-start = ((), (), s32[]{:S(2)}) async-start(), calls=%async_computation.14 | async-start | bytes 245760
  286.6 531.6 %reduce-scatter.25.cloned.1.call-start = ((), (), s32[]{:S(2)}) async-start(), calls=%async_computation.13 | async-start | bytes 737280
  419.0 402.5 %reduce-scatter.29.cloned.1.call-start = ((), (), s32[]{:S(2)}) async-start(), calls=%async_computation.15 | async-start | bytes 737280
  585.6 258.0 %reduce-scatter.21.cloned.1.call-start = ((), (), s32[]{:S(2)}) async-start(), calls=%async_computation.11 | async-start | bytes 737280 | tf_op jit(solution)/shard_map/reduce_scatter | solution.py:284
  590.9 158.9 %copy-start.53 = (f32[1,2,2,128]{3,1,2,0:T(2,128)S(1)}, f32[1,2,2,128]{3,1,2,0:T(2,128)}, u32[]{:S(2)}) copy-start(f32[1,2,2,128]{3,1,2,0:T(2,128)} %copy-done.52) | copy-start | bytes 6148
  590.9 158.9 %copy-start.55 = (f32[1,2,2,128]{3,1,2,0:T(2,128)S(1)}, f32[1,2,2,128]{3,1,2,0:T(2,128)}, u32[]{:S(2)}) copy-start(f32[1,2,2,128]{3,1,2,0:T(2,128)} %copy-done.54) | copy-start | bytes 6148
  749.9 6.0 copy-start.58
  749.9 61.4 %copy-start.57 = (f32[768]{0:T(1024)S(1)}, f32[768]{0:T(1024)}, u32[]{:S(2)}) copy-start(f32[768]{0:T(1024)} %param.39) | copy-start | bytes 9220
  (4 other events, 3.6 us)
Sparse Core Ops, SparseCore 0:
  181.7 101.4 reduce-scatter.16
  286.9 127.9 reduce-scatter.14
  418.9 162.3 reduce-scatter.22
  585.2 162.3 reduce-scatter.18
  750.6 18.8 reduce-scatter.26
  772.0 22.0 reduce-scatter.24
  796.8 22.0 reduce-scatter.28
  821.5 22.0 reduce-scatter.20
where the time goes:
time: 862 us; the launch traced here: 852 us
  waiting for transfers between devices  522 us (61%)
  matrix products  85.5 us (10%)
  local copies, waits for them, and re-layouts  70.7 us (8%)
  other arithmetic  60.4 us (7%)
  blocking collectives  43.2 us (5%)
  starting transfers between devices  38.9 us (5%)
  between operations  16.5 us (2%)
  loops' own time  15.1 us (2%)
    reduce_scatter x1, waiting for transfers between devices, body(): lax.psum_scatter(grad_wproj, 'dp', scatter_dimension=0, tiled=True)  162 us
    reduce_scatter x1, waiting for transfers between devices, body(): lax.psum_scatter(grad_wfc, 'dp', scatter_dimension=0, tiled=True)  146 us
    reduce_scatter x1, waiting for transfers between devices, body(): lax.psum_scatter(grad_wqkv, 'dp', scatter_dimension=0, tiled=True)  128 us
    ppermute x6, waiting for transfers between devices, shifted(): return lax.ppermute(shard, axis, pairs)  47.4 us
    ppermute x6, starting transfers between devices, shifted(): return lax.ppermute(shard, axis, pairs)  38 us
    unnamed x1, blocking collectives  36.8 us
    unnamed x133, local copies, waits for them, and re-layouts  33.8 us
    reduce_scatter x1, waiting for transfers between devices, body(): lax.psum_scatter(grad_wout, 'dp', scatter_dimension=0, tiled=True)  19 us
  transfers between devices with their start and end apart: 14, of which 9 were waited for; matrix products, arithmetic and copies ran while one was open for 17% of the time, Pallas kernels for 0%

commit v1 on v0

v1 whole, which is shorter than its diff:
```python
import functools

import jax
import jax.numpy as jnp
from jax import lax
from jax.experimental import pallas as pl
from jax.experimental.pallas import tpu as pltpu
from jax.sharding import PartitionSpec as P

HEADS = 12
HEAD = 64

ln_epsilon = 1e-05
gelu_factor = 0.7978845608028654
big_negative = -1e30

BF = jnp.bfloat16
F32 = jnp.float32
MESH = pl.DeviceIdType.MESH

SPAN = 256
BLOCKS = 4
SEQ = SPAN * BLOCKS
D = 768
HALF = D // 2
FF = 1536
CHUNK = 512
OWN = 96
EARLY = 56

PA_ORDER = ("x", "zh", "y")
PB_ORDER = ("zh", "y", "x")
FA_ORDER = ("zl", "y", "x", "zh")
FB_ORDER = ("y", "zl", "x", "zh")
WO_ORDER = ("y", "zl", "x")
Q_ORDER = ("x", "zl", "zh")
Q_CHAINS = ((0, 0, 3), (1, 0, 3), (2, 0, 1), (2, 1, 1), (2, 2, 1))


PLACES = (
    [("back", n) for n in range(2)]
    + ["branch"]
    + [("pair", p, i) for p in range(3) for i in (3, 2, 1, 0, -1)]
    + [("input", n) for n in range(2)]
    + ["last"]
)
STEPS = {
    "branch": ["pa", "ve"],
    ("pair", 0, 2): ["ve"],
    ("pair", 1, 2): ["ve"],
    ("pair", 1, 1): ["pb", "fa"],
    ("pair", 1, -1): ["fb", "q0"],
    ("pair", 2, 3): ["ve"],
    ("pair", 2, 2): ["pa", "ve"],
    ("pair", 2, -1): ["wo", "q1", "q0"],
    ("input", 1): ["fb"],
    "last": (
        ["q2a", "q2b", "q2c", "q0", "pa", "pa", "vl", "fb", "wo", "pb", "q1", "fa", "vl", "q0", "q0", "wo"]
        + ["q2a", "q2b", "q2c", "pa", "wo", "q2a", "q2b", "pb", "q2c", "fa", "fb", "q1", "pb", "q1", "pb", "wo"]
        + ["q1", "fa"]
    ),
}


def numbered(extras):
    seen, out = {}, {}
    for place in PLACES:
        names = list(STEPS.get(place, ()))
        if place == "last":
            names += ["ve"] * extras
        out[place] = []
        for name in names:
            out[place].append((name, seen.get(name, 0)))
            seen[name] = seen.get(name, 0) + 1
    return out


def proj_lands(order):
    rows, halves, shapes = D, 2, []
    for axis in order:
        if axis == "zh":
            halves = 1
        else:
            rows //= 2
        shapes.append((halves, rows, HALF))
    return shapes + [(2, OWN, HALF), (OWN, HALF)]


def fc_lands(order):
    rows, cols, shapes = D, D, []
    for axis in order:
        if axis == "y":
            cols //= 2
        else:
            rows //= 2
        shapes.append((rows, cols))
    return shapes


def row_lands(order, cols):
    return [(D >> (n + 1), cols) for n in range(len(order))]


def row_weights(order, last=1):
    return {axis: last << (len(order) - 1 - n) for n, axis in enumerate(order)}


def stats(v):
    centre = jnp.mean(v, axis=-1, keepdims=True)
    centered = v - centre
    inverse = lax.rsqrt(jnp.mean(centered * centered, axis=-1, keepdims=True) + ln_epsilon)
    return centered * inverse, inverse


def norm_back(grad_norm, normed, inverse):
    first = jnp.mean(grad_norm, axis=-1, keepdims=True)
    second = jnp.mean(grad_norm * normed, axis=-1, keepdims=True)
    return inverse * (grad_norm - first - normed * second)


def nn(a, b):
    return jnp.dot(a, b, preferred_element_type=F32)


def nt(a, b):
    return lax.dot_general(a, b, (((1,), (1,)), ((), ())), preferred_element_type=F32)


def mul(i, n):
    return pl.multiple_of(i * n, n)


def loop(n, body):
    def step(i, carry):
        body(i)
        return carry

    lax.fori_loop(0, n, step, 0)


def gelu_both(v):
    square = v * v
    inner = jnp.tanh(v * (gelu_factor + 0.044715 * gelu_factor * square))
    half = 0.5 + 0.5 * inner
    value = v * half
    return value, half + value * ((1.0 - inner) * (gelu_factor + 3.0 * 0.044715 * gelu_factor * square))


def top_of(v):
    while v.shape[0] > 8:
        half = v.shape[0] // 2
        v = jnp.maximum(v[:half], v[half:])
    return v


def base(i):
    return SPAN * (i * (i + 1) // 2)


def scratch(dp):
    extras = max(0, dp.bit_length() - 4)
    vm = pltpu.VMEM
    shapes = dict(
        xrow=vm((BLOCKS, SPAN, D), BF),
        drow=vm((BLOCKS, SPAN, D), BF),
        wqkv=vm((D, 3 * HALF), BF),
        wout=vm((D, D), BF),
        wfc=vm((D, FF), BF),
        wproj=vm((FF, D), BF),
        bfc=vm((1, FF), F32),
        ain_t=vm((D, SEQ), BF),
        qn=vm((SEQ, HALF), BF),
        kn=vm((SEQ, HALF), BF),
        vn=vm((SEQ, HALF), BF),
        k_t=vm((128, SEQ), BF),
        v_t=vm((6, HEAD + 16, SEQ), BF),
        start=vm((BLOCKS, 1, SPAN), jnp.int32),
        probs=vm((6, base(4), SPAN), BF),
        linv=vm((6, 1, SEQ), F32),
        delta=vm((6, 1, SEQ), F32),
        o_t=vm((HALF, SEQ), BF),
        mix=vm((2, SEQ, HALF), BF),
        gpj=vm((D, FF), BF),
        gfb=vm((D, D), BF),
        vectors=vm((1, 8 * D + 2 * FF), F32),
        dout_t=vm((D, SEQ), BF),
        hid=vm((SEQ, FF), BF),
        gpre=vm((SEQ, FF), BF),
        obuf=vm((2, SPAN, D), BF),
        oin=vm((2, SPAN, D), BF),
        gbuf=vm((2, SPAN, D), BF),
        gin=vm((2, SPAN, D), BF),
        gres=vm((2, SPAN, D), F32),
        gbr=vm((BLOCKS, SPAN, D), BF),
        dq_t=vm((128, SPAN), F32),
        dk=vm((SEQ, 128), F32),
        dv=vm((SEQ, 128), F32),
        acc_bfc=vm((1, FF), F32),
        acc_qv=vm((2, 1, HALF), F32),
        acc=vm((6, 1, D), F32),
        early=vm((6 + extras, EARLY, 128), F32),
        early_r=vm((5 + extras, EARLY, 128), F32),
        late=vm((dp, 8, 128), F32),
        late_r=vm((dp, 8, 128), F32),
        late_s=vm((8, 128), F32),
        late_q=vm((3, 8, 128), F32),
        late_send=pltpu.SemaphoreType.DMA((dp + 3,)),
        late_recv=pltpu.SemaphoreType.DMA((dp + 3,)),
        local=pltpu.SemaphoreType.DMA((16,)),
        send=pltpu.SemaphoreType.DMA((120,)),
        recv=pltpu.SemaphoreType.DMA((120,)),
    )
    lands = dict(
        pa=proj_lands(PA_ORDER),
        pb=proj_lands(PB_ORDER),
        fa=fc_lands(FA_ORDER),
        fb=fc_lands(FB_ORDER),
        wo=row_lands(WO_ORDER, HALF) + [(2, OWN, HALF), (OWN, HALF)],
    )
    for n, (_, _, units) in enumerate(Q_CHAINS):
        cols = 128 * units
        if n < 2:
            lands[f"q{n}"] = row_lands(Q_ORDER, cols) + [(OWN, cols)] * 3
        else:
            lands[f"q{n}"] = [(4 * OWN, cols), (3, OWN, cols), (3, OWN, cols)]
    for name, sizes in lands.items():
        for n, size in enumerate(sizes):
            shapes[f"{name}_{n}"] = vm(size, BF)
    if extras:
        shapes.update(
            xs_pj=vm((1, HALF // 2, HALF), BF),
            xr_pj=vm((extras, HALF // 2, HALF), BF),
            xs_fc=vm((1, OWN, D), BF),
            xr_fc=vm((extras, OWN, D), BF),
            xs_wo=vm((1, OWN, HALF), BF),
            xr_wo=vm((extras, OWN, HALF), BF),
            xs_q=vm((1, 3, OWN, HALF), BF),
            xr_q=vm((extras, 3, OWN, HALF), BF),
            xc_q=vm((3, OWN, HALF), BF),
            xsend=pltpu.SemaphoreType.DMA((extras, 4)),
            xrecv=pltpu.SemaphoreType.DMA((extras, 4)),
        )
    return shapes


VECTORS = ("b_query", "b_value", "b_out", "b_proj", "gain_one", "shift_one", "gain_two", "shift_two", "b_fc")
INPUTS = ("x_in", "lengths", "w_qkv", "w_out", "w_fc", "w_proj", "d_in") + tuple(n + "_in" for n in VECTORS)
OUTPUTS = ("y_out", "gx_out", "gq_out", "gwo_out", "gfc_out", "gpj_out", "early_out", "late_out")


def kernel(dp, names, *refs):
    r = dict(zip(names, refs))
    a = type("Refs", (), r)
    for n, name in enumerate(VECTORS):
        size = 2 * FF if name == "b_fc" else D
        a.vectors[:, D * n : D * n + size] = r[name + "_in"][...].reshape(1, size)
        setattr(a, name, a.vectors.at[:, D * n : D * n + size])
    d = lax.axis_index("dp")
    b = lax.axis_index("blk")
    y = lax.div(b, 2)
    c = lax.rem(b, 2)
    other = 1 - c

    def bit(weight):
        return lax.rem(lax.div(d, weight), 2)

    def across(weight):
        return (d + weight * (1 - 2 * bit(weight)), b)

    t2, t1, t0 = bit(dp // 2), bit(dp // 4), bit(dp // 8)
    to_core = (d, 2 * y + other)
    to_y = (d, 2 * (1 - y) + c)
    to2, to1, to0 = across(dp // 2), across(dp // 4), across(dp // 8)
    to21 = (to2[0] + to1[0] - d, b)
    to_diagonal = (d, 2 * (1 - y) + other)
    groups = [(lax.rem(d + n, dp), b) for n in range(1, dp)]
    extra = []
    weight = dp // 16
    while weight >= 1:
        extra.append(across(weight))
        weight //= 2

    count = [0]

    def numbers(n):
        count[0] += n
        return count[0] - n

    def remote(src, dst, number, device):
        return pltpu.make_async_remote_copy(
            src_ref=src,
            dst_ref=dst,
            send_sem=a.send.at[number],
            recv_sem=a.recv.at[number],
            device_id=device,
            device_id_type=MESH,
        )

    pending = []

    def post(src, dst, device):
        copy = remote(src, dst, numbers(1), device)
        copy.start()
        pending.append(copy)
        return copy

    barrier = pltpu.get_barrier_semaphore()
    partners = [to_core, to_y, to_diagonal] + groups
    for device in partners:
        pl.semaphore_signal(barrier, inc=1, device_id=device, device_id_type=MESH)
    pl.semaphore_wait(barrier, len(partners))

    far = 2 * (1 - y) + c
    near_p = 2 * y + other
    far_p = 2 * (1 - y) + other
    x_y = post(a.x_in.at[1 - y], a.xrow.at[b], to_y)
    x_c = post(a.x_in.at[y], a.xrow.at[b], to_core)
    x_l = pltpu.make_async_copy(a.x_in.at[y], a.xrow.at[b], a.local.at[0])
    x_l.start()
    half_c = mul(c, HALF)
    loads_qkv = []
    for u in range(3):
        loads_qkv.append(
            pltpu.make_async_copy(
                a.w_qkv.at[:, pl.ds(pl.multiple_of(D * u + c * HALF, 128), HALF)],
                a.wqkv.at[:, pl.ds(HALF * u, HALF)],
                a.local.at[1 + u],
            )
        )
    loads_mlp = [pltpu.make_async_copy(a.w_out, a.wout, a.local.at[4])]
    for h in range(2):
        ff_at = pl.ds(pl.multiple_of(h * FF + c * D, 128), D)
        loads_mlp.append(
            pltpu.make_async_copy(a.w_fc.at[:, ff_at], a.wfc.at[:, pl.ds(h * D, D)], a.local.at[5 + h])
        )
        loads_mlp.append(
            pltpu.make_async_copy(a.w_proj.at[ff_at], a.wproj.at[pl.ds(h * D, D)], a.local.at[7 + h])
        )
        a.bfc[:, h * D : h * D + D] = a.b_fc[:, ff_at]
    d_l = pltpu.make_async_copy(a.d_in.at[y], a.drow.at[b], a.local.at[9])
    for load in loads_qkv + [d_l] + loads_mlp:
        load.start()
    d_y = remote(a.d_in.at[1 - y], a.drow.at[b], numbers(1), to_y)
    pending.append(d_y)
    d_c = post(a.d_in.at[y], a.drow.at[b], to_core)

    position = lax.broadcasted_iota(jnp.int32, (1, SPAN), 1)
    for i in range(BLOCKS):
        begin = jnp.zeros((1, SPAN), jnp.int32)
        total = jnp.int32(0)
        for j in range(8):
            total = total + a.lengths[y, j]
            begin = jnp.where(position + SPAN * i >= total, total, begin)
        a.start[i] = begin
    a.acc[...] = jnp.zeros_like(a.acc)
    a.v_t[:, HEAD:, :] = jnp.ones((6, 16, SEQ), BF)

    for load in loads_qkv:
        load.wait()
    bias_q = a.b_query[:, pl.ds(half_c, HALF)]
    bias_v = a.b_value[:, pl.ds(half_c, HALF)]

    def project(t):
        rows = pl.ds(mul(t, SPAN), SPAN)
        normed, _ = stats(a.xrow[t].astype(F32))
        low = (normed * a.gain_one[...] + a.shift_one[...]).astype(BF)
        out = nn(low, a.wqkv[...])
        a.qn[rows, :] = ((out[:, :HALF] + bias_q).astype(BF).astype(F32) * 0.125).astype(BF)
        values = (out[:, 2 * HALF :] + bias_v).astype(BF)
        turned = values.T
        a.kn[rows, :] = out[:, HALF : 2 * HALF].astype(BF)
        a.vn[rows, :] = values
        for h in range(6):
            a.v_t[h, :HEAD, rows] = turned[HEAD * h : HEAD * h + HEAD]

    def turn(t):
        rows = pl.ds(mul(t, SPAN), SPAN)
        normed, _ = stats(a.xrow[t].astype(F32))
        a.ain_t[:, rows] = (normed * a.gain_one[...] + a.shift_one[...]).astype(BF).T

    def turn_d(t):
        a.dout_t[:, pl.ds(mul(t, SPAN), SPAN)] = a.drow[t].T

    def stack(ref, ts):
        return jnp.concatenate([ref[t] for t in ts], axis=0)

    def stack_rows(ref, spans, cols=slice(None)):
        return jnp.concatenate([ref[rows, cols] for rows in spans], axis=0)

    def spans_of(ts):
        return [pl.ds(mul(t, SPAN), SPAN) for t in ts]

    def grad_hidden(ts, slopes):
        spans = spans_of(ts)
        top = stack(a.drow, ts)
        for f in range(0, FF, CHUNK):
            here = slice(f, f + CHUNK)
            grad = nt(top, a.wproj[here, :])
            if slopes:
                grad = grad * stack_rows(a.gpre, spans, here).astype(F32)
            grad = grad.astype(BF)
            for k, rows in enumerate(spans):
                a.gpre[rows, here] = grad[SPAN * k : SPAN * k + SPAN]

    fwd_x = remote(a.xrow.at[far], a.xrow.at[far], numbers(1), to_core)
    fwd_d = remote(a.drow.at[far], a.drow.at[far], numbers(1), to_core)
    pending += [fwd_x, fwd_d]

    def arrive(s):
        @pl.when(s == 0)
        def _():
            x_l.wait()

        @pl.when(s == 1)
        def _():
            x_c.wait_recv()

        @pl.when(s == 2)
        def _():
            x_y.wait_recv()
            fwd_x.start()
            d_y.start()

        @pl.when(s == 3)
        def _():
            fwd_x.wait_recv()

        far_s = lax.div(s, 2)
        core_s = lax.rem(s, 2)
        t = 2 * (y + far_s * (1 - 2 * y)) + c + core_s * (1 - 2 * c)
        project(t)

        @pl.when(s == 0)
        def _():
            d_l.wait()

        @pl.when(s == 1)
        def _():
            d_c.wait_recv()

            for load in loads_mlp:
                load.wait()

        @pl.when(s < 2)
        def _():
            turn(t)
            turn_d(t)

        @pl.when(s == 1)
        def _():
            grad_hidden((b, near_p), False)

    loop(4, arrive)

    lane = lax.broadcasted_iota(jnp.int32, (1, 128), 1)
    key_index = lax.broadcasted_iota(jnp.int32, (SPAN, SPAN), 0)
    query_index = lax.broadcasted_iota(jnp.int32, (SPAN, SPAN), 1)
    mix_first = numbers(3)

    def mix_copy(p):
        here = a.mix.at[c, :, pl.ds(mul(p, 128), 128)]
        return remote(here, here, mix_first + p, to_core)

    def forward_pair(p):
        cols = pl.ds(mul(p, 128), 128)
        for i in range(BLOCKS):
            rows = slice(SPAN * i, SPAN * i + SPAN)
            keys_n = SPAN * (i + 1)
            pair = a.qn[rows, cols]
            begin = a.start[i]
            for e in range(2):
                head = 2 * p + e
                query = jnp.where(lane // HEAD == e, pair, jnp.zeros_like(pair))
                scores, tops = [], []
                product = nt(a.kn[:keys_n, cols], query)
                for j in range(i + 1):
                    s = product[SPAN * j : SPAN * j + SPAN]
                    ok = key_index + SPAN * j >= begin
                    if j == i:
                        ok = ok & (key_index <= query_index)
                    s = jnp.where(ok, s, big_negative)
                    scores.append(s)
                    tops.append(top_of(s))
                top = tops[0]
                for here in tops[1:]:
                    top = jnp.maximum(top, here)
                top = jnp.max(top, axis=0, keepdims=True)
                for j in range(i + 1):
                    at = base(i) + SPAN * j
                    a.probs[head, at : at + SPAN, :] = jnp.exp(scores[j] - top).astype(BF)

        def mix_head(e):
            head = 2 * p + e
            feats = pl.ds(mul(head, HEAD), HEAD)
            for i in range(BLOCKS):
                rows = slice(SPAN * i, SPAN * i + SPAN)
                keys_n = SPAN * (i + 1)
                out = nn(a.v_t[head, :, :keys_n], a.probs[head, base(i) : base(i) + keys_n, :])
                inverse = 1.0 / out[HEAD : HEAD + 1]
                a.linv[head, :, rows] = inverse
                a.o_t[feats, rows] = (out[:HEAD] * inverse).astype(BF)

        loop(2, mix_head)
        a.mix[c, :, cols] = a.o_t[pl.ds(mul(p, 128), 128), :].T
        mix_copy(p).start()

        @pl.when(p == 2)
        def _():
            d_y.wait_recv()
            fwd_d.start()

    loop(3, forward_pair)
    turn(far)
    turn(far_p)

    for p in range(3):
        mix_copy(p).wait_recv()

    o_first, g_first, b_first = numbers(2), numbers(2), numbers(2)

    def o_copy(s):
        return remote(a.obuf.at[s], a.oin.at[s], o_first + s, to_core)

    def g_copy(s):
        return remote(a.gbuf.at[s], a.gin.at[s], g_first + s, to_core)

    def b_copy(k):
        t = far if k else b
        return remote(a.gbr.at[t], a.gbr.at[t], b_first + k, to_core)

    y_far = remote(a.gbuf.at[1], a.y_out.at[y], numbers(1), to_y)
    y_own = pltpu.make_async_copy(a.gbuf.at[0], a.y_out.at[y], a.local.at[10])

    def blocks_of(g):
        core = other + g * (2 * c - 1)
        return 2 * y + core, 2 * (1 - y) + core

    def layer_pair(g):
        ts = blocks_of(g)
        spans = spans_of(ts)
        mixed = jnp.concatenate([stack_rows(a.mix.at[n], spans) for n in range(2)], axis=1)
        residual = stack(a.xrow, ts).astype(F32) + nn(mixed, a.wout[...]) + a.b_out[...]
        normed, _ = stats(residual)
        low = (normed * a.gain_two[...] + a.shift_two[...]).astype(BF)
        for k, rows in enumerate(spans):
            a.wqkv[:, rows] = low[SPAN * k : SPAN * k + SPAN].T
        for f in range(0, FF, CHUNK):
            here = slice(f, f + CHUNK)
            value, slope = gelu_both(nn(low, a.wfc[:, here]) + a.bfc[:, here])
            value = value.astype(BF)
            a.hid[spans[0], here] = value[:SPAN]
            a.hid[spans[1], here] = value[SPAN:]
            a.gpre[spans[0], here] = (slope[:SPAN] * a.gpre[spans[0], here].astype(F32)).astype(BF)
            a.gpre[spans[1], here] = slope[SPAN:].astype(BF)

        @pl.when(g == 1)
        def _():
            a.gres[0] = residual[:SPAN]
            a.gres[1] = residual[SPAN:]

    loop(2, layer_pair)
    fwd_d.wait_recv()
    turn_d(far)
    turn_d(far_p)

    def part(first, size, n=1):
        return pl.ds(pl.multiple_of(first * size, size), n * size)

    class Chain:
        def __init__(self, stages):
            self.stages = [one_copy(*stage) if len(stage) == 4 else stage for stage in stages]
            self.first = [numbers(len(stage[0])) for stage in self.stages]

        def copies(self, k):
            pieces, _, device = self.stages[k]
            made = [piece() for piece in pieces]
            return [
                remote(piece[0], piece[1], self.first[k] + n, piece[2] if device is None else device)
                for n, piece in enumerate(made)
            ]

        def start(self, k):
            for copy in self.copies(k):
                copy.start()

        def arrive(self, k):
            for copy in self.copies(k):
                copy.wait_recv()

        def step(self, k):
            self.arrive(k)
            keep = self.stages[k][1]
            if keep is not None:
                keep()
            self.start(k + 1)

        def sent(self):
            for k in range(len(self.stages)):
                for copy in self.copies(k):
                    copy.wait_send()

    def plus(keep, came):
        kept, landed = keep(), came()
        kept[...] = kept[...] + landed[...]

    def one_copy(out, land, keep, device):
        landing = land if callable(land) else lambda: land
        return [lambda: (out(), landing())], (lambda: plus(keep, landing)) if keep else None, device

    axes = dict(x=(t0, to0), zl=(t1, to1), zh=(t2, to2), y=(y, to_y))

    def lands_of(name, n):
        return [r[f"{name}_{k}"] for k in range(n)]

    def proj_chain(name, first, order):
        lands = lands_of(name, 5)
        own, last = lands[3], lands[4]

        def at(block, n, h):
            rows = pl.ds(pl.multiple_of(OWN * block, OWN), OWN * n)
            return a.gpj.at[rows, pl.ds(pl.multiple_of(D * h + first, HALF), HALF)]

        stages = []
        start, width, halves = 0, 8, (0, 1)
        for k, axis in enumerate(order):
            mine, device = axes[axis]
            if axis == "zh":
                pairs = [(start, width, 1 - mine, start, mine)]
                halves = (mine,)
            else:
                width //= 2
                gone, kept = start + (1 - mine) * width, start + mine * width
                pairs = [(gone, width, h, kept, h) for h in halves]
                start = kept
            pieces = [
                lambda p=p, k=k, n=n: (at(p[0], p[1], p[2]), lands[k].at[n]) for n, p in enumerate(pairs)
            ]

            def keep(pairs=pairs, k=k, final=k == len(order) - 1, start=start):
                for n, p in enumerate(pairs):
                    plus(lambda: at(p[3], p[1], p[4]), lambda: lands[k].at[n])
                if final:
                    own[c] = at(start + c, 1, t2)[...]

            stages.append((pieces, keep, device))
        stages.append(([lambda: (at(start + other, 1, t2), own.at[c])], None, to_core))
        stages.append(([lambda: (own.at[1 - t1], last)], None, to1))
        return Chain(stages)

    pa = proj_chain("pa", 0, PA_ORDER)
    pb = proj_chain("pb", HALF, PB_ORDER)

    def fc_chain(name, buf, order):
        lands = lands_of(name, 4)

        def at(block, n, w):
            rows = pl.ds(pl.multiple_of(OWN * block, OWN), OWN * n)
            if w is None:
                return buf.at[rows, pl.ds(0, D)]
            return buf.at[rows, part(w, HALF)]

        stages = []
        start, width, side = 0, 8, None
        for k, axis in enumerate(order):
            mine, device = axes[axis]
            if axis == "y":
                gone, kept = (start, width, 1 - y), (start, width, y)
                side = y
            else:
                width //= 2
                gone, kept = (start + (1 - mine) * width, width, side), (start + mine * width, width, side)
                start = kept[0]
            final = k == len(order) - 1
            stages.append(
                (
                    lambda gone=gone: at(*gone),
                    lands[k],
                    None if final else lambda kept=kept: at(*kept),
                    device,
                )
            )
        return Chain(stages), lambda: at(start, 1, y), lands[-1]

    fa, fa_own, fa_last = fc_chain("fa", a.dout_t, FA_ORDER)
    fb, fb_own, fb_last = fc_chain("fb", a.gfb, FB_ORDER)

    def row_stages(at, order, lands):
        stages = []
        start, width = 0, 8
        for k, axis in enumerate(order):
            mine, device = axes[axis]
            width //= 2
            gone, kept = start + (1 - mine) * width, start + mine * width
            stages.append(
                (
                    lambda gone=gone, width=width: at(gone, width),
                    lands[k],
                    lambda kept=kept, width=width: at(kept, width),
                    device,
                )
            )
            start = kept
        return stages, lambda: at(start, 1)

    wo_lands = lands_of("wo", 5)
    wo_stages, wo_own = row_stages(
        lambda block, n: a.wout.at[pl.ds(pl.multiple_of(OWN * block, OWN), OWN * n), pl.ds(0, HALF)],
        WO_ORDER,
        wo_lands,
    )

    def wo_keep():
        kept = wo_own()
        total = (kept[...].astype(F32) + wo_lands[2][...].astype(F32)).astype(BF)
        kept[...] = total
        wo_lands[3][c] = total

    wo = Chain(
        wo_stages[:2]
        + [
            ([lambda: (wo_stages[2][0](), wo_lands[2])], wo_keep, wo_stages[2][3]),
            (wo_own, lambda: wo_lands[3].at[c], None, to_core),
            (lambda: wo_lands[3].at[1 - t2], wo_lands[4], None, to2),
        ]
    )

    def q_chain(n):
        p, first, units = Q_CHAINS[n]
        cols = slice(HALF * p + 128 * first, HALF * p + 128 * (first + units))

        def at(block, n_blocks):
            return a.gpre.at[pl.ds(pl.multiple_of(OWN * block, OWN), OWN * n_blocks), cols]

        def put(core, value):
            a.gq_out[core, p, :, pl.ds(128 * first, 128 * units)] = value

        if n >= 2:
            came_x, came_z, came = lands_of(f"q{n}", 3)
            start = 4 * t0
            own = lambda: at(start + 2 * t1 + t2, 1)
            around = ((2 * (1 - t1) + t2, to1), (2 * t1 + 1 - t2, to2), (2 * (1 - t1) + 1 - t2, to21))

            def keep_z():
                total = own()[...].astype(F32)
                for m in range(3):
                    total = total + came_z[m].astype(F32)
                own()[...] = total.astype(BF)

            def finish():
                chain.arrive(2)
                put(c, own()[...] + came[0])
                put(other, came[1] + came[2])

            chain = Chain(
                [
                    (lambda: at(4 * (1 - t0), 4), came_x, lambda: at(start, 4), to0),
                    (
                        [
                            lambda m=m, block=block, device=device: (at(start + block, 1), came_z.at[m], device)
                            for m, (block, device) in enumerate(around)
                        ],
                        keep_z,
                        None,
                    ),
                    (
                        [
                            lambda m=m, device=device: (own(), came.at[m], device)
                            for m, device in enumerate((to_y, to_core, to_diagonal))
                        ],
                        None,
                        None,
                    ),
                ]
            )
            return chain, finish
        lands = lands_of(f"q{n}", 6)
        stages, own = row_stages(at, Q_ORDER, lands)

        def keep_y():
            lands[5][...] = own()[...] + lands[3][...]

        def finish():
            chain.arrive(4)
            put(c, lands[5][...])
            put(other, lands[4][...])

        chain = Chain(
            stages + [([lambda: (own(), lands[3])], keep_y, to_y), (lambda: lands[5], lands[4], None, to_core)]
        )
        return chain, finish

    def vector_chain(buf, came):
        def stage(n, device):
            def keep():
                buf[n + 1] = buf[n] + came[n]

            return [lambda: (buf.at[n], came.at[n])], keep, device

        return Chain([stage(n, device) for n, device in enumerate([to0, to1, to2, to_y, to_core] + extra)])

    ve = vector_chain(a.early, a.early_r)

    def late_copy(src, dst, number, device):
        return pltpu.make_async_remote_copy(
            src_ref=src,
            dst_ref=dst,
            send_sem=a.late_send.at[number],
            recv_sem=a.late_recv.at[number],
            device_id=device,
            device_id_type=MESH,
        )

    def late_groups():
        return [late_copy(a.late.at[to[0]], a.late_r.at[n + 1], n, to) for n, to in enumerate(groups)]

    def late_row():
        row = (to_core, to_y, to_diagonal)
        return [late_copy(a.late_s, a.late_q.at[n], dp - 1 + n, to) for n, to in enumerate(row)]

    def late_share():
        for copy in late_groups():
            copy.wait_recv()
        total = a.late[d]
        for n in range(1, dp):
            total = total + a.late_r[n]
        a.late_s[...] = total
        for copy in late_row():
            copy.start()

    def late_end():
        for copy in late_row():
            copy.wait_recv()
        a.late_out[...] = a.late_s[...] + a.late_q[0] + a.late_q[1] + a.late_q[2]

    qs = [q_chain(n) for n in range(len(Q_CHAINS))]

    def finish(chain, out, keep, land):
        chain.arrive(len(chain.stages) - 1)
        out[...] = keep[...].astype(F32) + land[...].astype(F32)

    chains = dict(pa=pa, pb=pb, fa=fa, fb=fb, wo=wo, ve=ve)
    last_steps = dict(
        pa=lambda: finish(pa, a.gpj_out.at[pl.ds(0, OWN)], r["pa_3"].at[t1], r["pa_4"]),
        pb=lambda: finish(pb, a.gpj_out.at[pl.ds(OWN, OWN)], r["pb_3"].at[t1], r["pb_4"]),
        fa=lambda: finish(fa, a.gfc_out.at[:, pl.ds(0, HALF)], fa_own(), fa_last),
        fb=lambda: finish(fb, a.gfc_out.at[:, pl.ds(HALF, HALF)], fb_own(), fb_last),
        wo=lambda: finish(wo, a.gwo_out, wo_lands[3].at[t2], wo_lands[4]),
        ve=lambda: (ve.arrive(len(ve.stages) - 1), ve.stages[-1][1]()),
    )
    for n, name in enumerate(("q0", "q1", "q2a", "q2b", "q2c")):
        chains[name], last_steps[name] = qs[n]
    plan = numbered(len(extra))
    assert sum(len(todo) for todo in plan.values()) == 2 + sum(len(chain.stages) for chain in chains.values())

    def steps(place):
        for name, k in plan[place]:
            if name == "vl":
                (late_share, late_end)[k]()
            elif k == len(chains[name].stages) - 1:
                last_steps[name]()
            else:
                chains[name].step(k)

    pa_w, pb_w = (row_weights([x for x in order if x != "zh"], 2) for order in (PA_ORDER, PB_ORDER))
    fa_w, fb_w = (row_weights([x for x in order if x != "y"]) for order in (FA_ORDER, FB_ORDER))
    wo_w, q_w = row_weights(WO_ORDER), row_weights(Q_ORDER)

    for n in range(2):
        h = (1 - t2) if n == 0 else t2
        for w in range(2):
            grad = nn(a.dout_t[HALF * w : HALF * w + HALF, :], a.hid[:, part(h, D)]).astype(BF)
            for i in range(2):
                for e in range(2):
                    piece = grad[2 * OWN * e : 2 * OWN * e + 2 * OWN, HALF * i : HALF * i + HALF]
                    at_a = OWN * (pa_w["x"] * i + pa_w["y"] * w + e)
                    at_b = OWN * (pb_w["x"] * i + pb_w["y"] * w + e)
                    a.gpj[at_a : at_a + OWN, pl.ds(pl.multiple_of(D * h, HALF), HALF)] = piece[:OWN]
                    a.gpj[at_b : at_b + OWN, pl.ds(pl.multiple_of(D * h + HALF, HALF), HALF)] = piece[OWN:]
        if n == 0:
            pb.start(0)
    pa.start(0)

    grad_hidden((far, far_p), True)

    def out_of(g):
        return nn(stack_rows(a.hid, spans_of(blocks_of(g))), a.wproj[...])

    def back_of(g):
        return nt(stack_rows(a.gpre, spans_of(blocks_of(g))), a.wfc[...])

    @pl.when(d >= 0)
    def _():
        out, grad = out_of(0), back_of(0)
        for k in range(2):
            a.obuf[k] = out[SPAN * k : SPAN * k + SPAN].astype(BF)
            o_copy(k).start()
        for k in range(2):
            a.gbuf[k] = grad[SPAN * k : SPAN * k + SPAN].astype(BF)
            g_copy(k).start()

    def weights_fc(n):
        h = lax.rem(n, 2)
        w = lax.div(n, 2)
        ones = jnp.ones((16, SEQ), BF)
        grad = nn(jnp.concatenate([a.wqkv[part(h, HALF), :SEQ], ones], axis=0), a.gpre[:, part(w, D)])
        a.acc_bfc[:, part(w, D)] = grad[HALF : HALF + 1]
        grad = grad.astype(BF)
        for j in range(2):
            for i in range(2):
                piece = grad[OWN * (2 * j + i) : OWN * (2 * j + i) + OWN]
                at_a = fa_w["x"] * i + fa_w["zl"] * j + fa_w["zh"] * h
                at_b = fb_w["x"] * i + fb_w["zl"] * j + fb_w["zh"] * h
                a.dout_t[part(at_a, OWN), part(w, HALF)] = piece[:, :HALF]
                a.gfb[part(at_b, OWN), part(w, HALF)] = piece[:, HALF:]

    loop(4, weights_fc)
    fa.start(0)
    fb.start(0)
    for load in loads_qkv:
        load.start()
    steps(("back", 0))

    @pl.when(d >= 0)
    def _():
        grad_in = back_of(1)
        for k in (1, 0):
            t = blocks_of(1)[k]
            normed, inverse = stats(a.gres[k])
            g_copy(k).wait_recv()
            grad = grad_in[SPAN * k : SPAN * k + SPAN] + a.gin[k].astype(F32)
            wide = a.drow[t].astype(F32)
            branch = (wide + norm_back(grad * a.gain_two[...], normed, inverse)).astype(BF)
            a.gbr[t] = branch
            b_copy(k).start()
            a.acc[0] += jnp.sum(branch.astype(F32), axis=0, keepdims=True)
            a.acc[1] += jnp.sum(wide, axis=0, keepdims=True)
            a.acc[4] += jnp.sum(grad * normed, axis=0, keepdims=True)
            a.acc[5] += jnp.sum(grad, axis=0, keepdims=True)

    steps(("back", 1))

    @pl.when(d >= 0)
    def _():
        out = out_of(1)
        for k in (1, 0):
            o_copy(k).wait_recv()
            g_copy(k).wait_send()
            whole = a.gres[k] + (out[SPAN * k : SPAN * k + SPAN] + a.oin[k].astype(F32)) + a.b_proj[...]
            a.gbuf[k] = whole.astype(BF)
            if k == 1:
                y_far.start()
            else:
                y_own.start()


    def pack(rows, vectors):
        pieces = [v[:, 128 * i : 128 * i + 128] for v in vectors for i in range(v.shape[1] // 128)]
        pieces += [jnp.zeros((1, 128), F32)] * (rows - len(pieces))
        return jnp.concatenate(pieces, axis=0)

    a.early[0] = jnp.zeros((EARLY, 128), F32)
    a.early[0, :24, :] = pack(24, [a.acc[n] for n in (0, 1, 4, 5)])
    a.early[0, pl.ds(pl.multiple_of(24 + 16 * c, 8), 16), :] = pack(16, [a.acc_bfc[...]])
    ve.start(0)

    b_copy(0).wait_recv()
    b_copy(1).wait_recv()

    def branch_block(t):
        rows = pl.ds(mul(t, SPAN), SPAN)
        grad = nt(a.wout[pl.ds(half_c, HALF), :], a.gbr[t])
        for p in range(3):
            parts = []
            for e in range(2):
                head = 2 * p + e
                at = slice(HEAD * head, HEAD * head + HEAD)
                inverse = a.linv[head, :, rows]
                piece = grad[at].astype(BF).astype(F32)
                a.delta[head, :, rows] = inverse * jnp.sum(
                    piece * a.o_t[at, rows].astype(F32), axis=0, keepdims=True
                )
                parts.append(piece * inverse)
            scaled = jnp.concatenate(parts, axis=0).astype(BF)
            a.hid[rows, 3 * HALF + 128 * p : 3 * HALF + 128 * p + 128] = scaled.T

    loop(4, branch_block)

    steps("branch")
    for n in range(2):
        lhs = a.o_t[2 * OWN * n : 2 * OWN * n + 2 * OWN, :]
        grad = nn(lhs[:, :SPAN], a.gbr[0])
        for t in range(1, BLOCKS):
            grad += nn(lhs[:, SPAN * t : SPAN * t + SPAN], a.gbr[t])
        grad = grad.astype(BF)
        for i in range(2):
            for w in range(2):
                at = OWN * (wo_w["zl"] * n + wo_w["x"] * i + wo_w["y"] * w)
                a.wout[at : at + OWN, :HALF] = grad[OWN * i : OWN * i + OWN, HALF * w : HALF * w + HALF]
    wo.start(0)

    def between(p, i):
        for value in range(3):
            if plan["pair", value, i]:

                @pl.when(p == value)
                def _():
                    steps(("pair", value, i))

    def backward_pair(p):
        cols = pl.ds(mul(p, 128), 128)
        do_cols = pl.ds(pl.multiple_of(3 * HALF + 128 * p, 128), 128)
        a.k_t[...] = a.kn[:, cols].T
        for i in reversed(range(BLOCKS)):
            rows = slice(SPAN * i, SPAN * i + SPAN)
            keys_n = SPAN * (i + 1)
            pair = a.qn[rows, cols]
            do_pair = a.hid[rows, do_cols]

            def grad_scores(e):
                head = 2 * p + e
                mine = (lane >= HEAD * e) & (lane < HEAD * e + HEAD)
                delta = a.delta[head, :, rows]
                product = nt(a.vn[:keys_n, cols], jnp.where(mine, do_pair, jnp.zeros_like(do_pair)))
                for j in range(i + 1):
                    at = base(i) + SPAN * j
                    keys = slice(SPAN * j, SPAN * j + SPAN)
                    weights = a.probs[head, at : at + SPAN, :].astype(F32)
                    low = (weights * (product[keys] - delta)).astype(BF)
                    a.mix[e, keys, :SPAN] = low

            def grad_query(e):
                low = a.mix[e, :keys_n, :SPAN]
                feats = pl.ds(mul(e, HEAD), HEAD)
                a.dq_t[feats, :] = nn(a.k_t[feats, :keys_n], low) * 0.125

            loop(2, grad_scores)
            loop(2, grad_query)
            a.hid[rows, cols] = a.dq_t[...].T.astype(BF)
            masks = [lane < HEAD, lane >= HEAD]
            query_both = jnp.concatenate([jnp.where(m, pair, jnp.zeros_like(pair)) for m in masks], axis=0)
            grad_both = jnp.concatenate([jnp.where(m, do_pair, jnp.zeros_like(pair)) for m in masks], axis=0)
            keys = slice(0, keys_n)
            at = base(i)
            scores = jnp.concatenate([a.mix[n, keys, :SPAN] for n in range(2)], axis=1)
            weights = jnp.concatenate(
                [a.probs[2 * p, at : at + keys_n, :], a.probs[2 * p + 1, at : at + keys_n, :]], axis=1
            )
            part_k = nn(scores, query_both)
            part_v = nn(weights, grad_both)
            if i == BLOCKS - 1:
                a.dk[...] = part_k
                a.dv[...] = part_v
            else:
                a.dk[keys, :] += part_k
                a.dv[keys, :] += part_v
            between(p, i)
        at_k = pl.ds(pl.multiple_of(HALF + 128 * p, 128), 128)
        at_v = pl.ds(pl.multiple_of(2 * HALF + 128 * p, 128), 128)
        low_k, low_v = a.dk[...].astype(BF), a.dv[...].astype(BF)
        a.hid[:, at_k] = low_k
        a.hid[:, at_v] = low_v

        @pl.when(p >= 0)
        def _():
            both = jnp.concatenate([a.hid[:, cols], a.hid[:, at_k], a.hid[:, at_v]], axis=1)
            ones = jnp.ones((16, SEQ), BF)
            grad = nn(jnp.concatenate([a.ain_t[...], ones], axis=0), both)
            a.acc_qv[0, :, cols] = grad[D : D + 1, :128]
            a.acc_qv[1, :, cols] = grad[D : D + 1, SPAN:]
            grad = grad.astype(BF)
            for h in range(2):
                for j in range(2):
                    for i in range(2):
                        at = (4 * h + 2 * j + i) * OWN
                        to = q_w["zh"] * h + q_w["zl"] * j + q_w["x"] * i
                        a.gpre[OWN * to : OWN * to + OWN, part(p, HALF)] = grad[at : at + OWN]

        for n, (pair, _, _) in enumerate(Q_CHAINS):

            @pl.when(p == pair)
            def _():
                qs[n][0].start(0)

        between(p, -1)

    for p in range(3):
        mix_copy(p).wait_send()
    loop(3, backward_pair)

    a_first = numbers(2)
    for load in loads_qkv:
        load.wait()

    def a_copy(s):
        return remote(a.obuf.at[s], a.oin.at[s], a_first + s, to_core)

    x_far = remote(a.gbuf.at[1], a.gx_out.at[y], numbers(1), to_y)
    x_own = pltpu.make_async_copy(a.gbuf.at[0], a.gx_out.at[y], a.local.at[11])

    def input_pair(g):
        ts = blocks_of(g)
        spans = spans_of(ts)
        part_in = nt(stack_rows(a.hid, spans, slice(0, 3 * HALF)), a.wqkv[...])
        for k in (1, 0):
            half = slice(SPAN * k, SPAN * k + SPAN)
            if g == 0:
                a.obuf[k] = part_in[half].astype(BF)
                a_copy(k).start()
                continue
            normed, inverse = stats(a.xrow[ts[k]].astype(F32))
            a_copy(k).wait_recv()
            grad = part_in[half] + a.oin[k].astype(F32)
            total = a.gbr[ts[k]].astype(F32) + norm_back(grad * a.gain_one[...], normed, inverse)
            a.gbuf[k] = total.astype(BF)
            if k == 1:
                x_far.start()
            else:
                x_own.start()
            a.acc[2] += jnp.sum(grad * normed, axis=0, keepdims=True)
            a.acc[3] += jnp.sum(grad, axis=0, keepdims=True)

    y_far.wait()
    y_own.wait()
    for k in range(2):
        o_copy(k).wait_send()

    for g in range(2):
        input_pair(g)
        steps(("input", g))

    share, half_dp = D // dp, dp // 2
    for e in range(dp):
        mine = (c == e // half_dp).astype(F32)
        at, at_half = share * e, share * (e % half_dp)
        rows = [a.acc[2, :, at : at + share], a.acc[3, :, at : at + share]]
        rows += [a.acc_qv[n, :, at_half : at_half + share] * mine for n in range(2)]
        tile = jnp.concatenate(rows + [jnp.zeros((4, share), F32)], axis=0)
        a.late[e] = jnp.concatenate([tile, jnp.zeros((8, 128 - share), F32)], axis=1)
    for copy in late_groups():
        copy.start()
    steps("last")

    for n, device in enumerate(extra):
        outs = (
            (a.gpj_out, a.xs_pj, a.xr_pj),
            (a.gfc_out, a.xs_fc, a.xr_fc),
            (a.gwo_out, a.xs_wo, a.xr_wo),
        )
        copies = []
        for m, (out, sent, came) in enumerate(outs):
            sent[0] = out[...].astype(BF)
            copies.append((out, sent, came, m))
        a.xs_q[0] = a.gq_out[c].astype(BF)
        copies.append((a.gq_out.at[c], a.xs_q, a.xr_q, 3))
        started = []
        for out, sent, came, m in copies:
            copy = pltpu.make_async_remote_copy(
                src_ref=sent.at[0],
                dst_ref=came.at[n],
                send_sem=a.xsend.at[n, m],
                recv_sem=a.xrecv.at[n, m],
                device_id=device,
                device_id_type=MESH,
            )
            copy.start()
            started.append(copy)
        for (out, sent, came, m), copy in zip(copies, started):
            copy.wait()
            out[...] = (sent[0].astype(F32) + came[n].astype(F32)).astype(out.dtype)
    if extra:
        a.xs_q[0] = a.gq_out[c]
        copy = remote(a.xs_q.at[0], a.xc_q, numbers(1), to_core)
        copy.start()
        copy.wait()
        a.gq_out[other] = a.xc_q[...]
    a.early_out[...] = a.early[5 + len(extra)]

    for copy in pending:
        copy.wait_send()
    for chain in chains.values():
        chain.sent()
    for s in range(2):
        a_copy(s).wait_send()
    b_copy(0).wait_send()
    b_copy(1).wait_send()
    for copy in (x_far, x_own):
        copy.wait()
    for copy in late_groups() + late_row():
        copy.wait_send()
    assert count[0] <= 120


def finish_kernel(dp, *refs):
    y_in, gx, gq, gwo, gfc, gpj, early, late = refs[:8]
    (y_out, gx_out, gq_out, bq_out, bv_out, gwo_out, bo_out, gfc_out, bf_out, gpj_out) = refs[8:18]
    rest = refs[18:]
    d = lax.axis_index("dp")
    b = lax.axis_index("blk")
    y, c = lax.div(b, 2), lax.rem(b, 2)
    subs = dp // 8
    sub = lax.rem(d, subs)
    rows = D // dp

    def rows_of(v):
        out = v[:rows]
        for n in range(1, subs):
            out = jnp.where(sub == n, v[rows * n : rows * n + rows], out)
        return out

    y_out[...] = y_in[...]
    gx_out[...] = gx[...].astype(F32)

    @pl.when(pl.program_id(0) == 0)
    def _():
        query = [jnp.concatenate([gq[n, p, :, :128] for p in range(3)], axis=1) for n in range(2)]
        key = [jnp.concatenate([gq[n, p, :, 128:256] for p in range(3)], axis=1) for n in range(2)]
        value = [jnp.concatenate([gq[n, p, :, 256:] for p in range(3)], axis=1) for n in range(2)]
        first = jnp.concatenate([query[0], query[1], key[0]], axis=1)
        second = jnp.concatenate([key[1], value[0], value[1]], axis=1)
        full = jnp.where(y == 0, first, second)
        columns = 3 * D // BLOCKS
        full = full.astype(F32)
        gq_out[...] = rows_of(jnp.where(c == 0, full[:, :columns], full[:, columns:]))
        columns = D // BLOCKS
        gwo_out[...] = rows_of(jnp.where(c == 0, gwo[:, :columns], gwo[:, columns:]))
        gfc_out[...] = rows_of(gfc[...])
        cols_ff = 2 * FF // dp
        out = gpj[:, :cols_ff]
        for n in range(1, subs):
            out = jnp.where(sub == n, gpj[:, cols_ff * n : cols_ff * n + cols_ff], out)
        gpj_out[...] = out

        def line(vec, first_row, n):
            return [vec[first_row + i : first_row + i + 1, :] for i in range(n)]

        def put(out, pieces):
            whole = jnp.concatenate(pieces, axis=1)
            size = whole.shape[1]
            n = size // dp
            turned = pltpu.roll(jnp.broadcast_to(whole, (8, size)), lax.rem(size - d * n, size), 1)
            out[...] = turned[0, :n]

        bq_out[...] = late[2, :rows]
        bv_out[...] = late[3, :rows]
        put(bo_out, line(early, 0, 6))
        put(bf_out, line(early, 24, 6) + line(early, 40, 6) + line(early, 30, 6) + line(early, 46, 6))
        for out, first_row in zip((rest[0], rest[3], rest[4]), (6, 12, 18)):
            put(out, line(early, first_row, 6))
        rest[1][...] = late[0, :rows]
        rest[2][...] = late[1, :rows]


def body(dp, layer_input, lengths, w_qkv, b_query, b_value, w_out, b_out, w_fc, b_fc, w_proj, b_proj, *more):
    d_out = more[4]
    vectors = (b_query, b_value, b_out, b_proj) + more[:4] + (b_fc,)
    args = (layer_input, lengths, w_qkv, w_out, w_fc, w_proj, d_out) + vectors
    shapes = scratch(dp)
    spaces = [pl.ANY, pltpu.SMEM] + [pl.ANY] * 5 + [pltpu.VMEM] * len(VECTORS)
    in_specs = [pl.BlockSpec(memory_space=space) for space in spaces]
    out_shape = (
        jax.ShapeDtypeStruct((2, SPAN, D), BF),
        jax.ShapeDtypeStruct((2, SPAN, D), BF),
        jax.ShapeDtypeStruct((2, 3, OWN, HALF), BF),
        jax.ShapeDtypeStruct((OWN, HALF), F32),
        jax.ShapeDtypeStruct((OWN, D), F32),
        jax.ShapeDtypeStruct((HALF // 2, HALF), F32),
        jax.ShapeDtypeStruct((EARLY, 128), F32),
        jax.ShapeDtypeStruct((8, 128), F32),
    )
    out_specs = [pl.BlockSpec(memory_space=pl.ANY)] * 2 + [pl.BlockSpec(memory_space=pltpu.VMEM)] * 6
    outs = pl.pallas_call(
        functools.partial(kernel, dp, INPUTS + OUTPUTS + tuple(shapes)),
        out_shape=out_shape,
        in_specs=in_specs,
        out_specs=out_specs,
        scratch_shapes=list(shapes.values()),
        compiler_params=pltpu.CompilerParams(
            collective_id=0, has_side_effects=True, vmem_limit_bytes=63 * 1024 * 1024
        ),
    )(*args)
    rows = D // dp
    line = jax.ShapeDtypeStruct((rows,), F32)
    out_shape = (
        jax.ShapeDtypeStruct((2, SPAN, D), BF),
        jax.ShapeDtypeStruct((2, SPAN, D), F32),
        jax.ShapeDtypeStruct((rows, 3 * D // BLOCKS), F32),
        line,
        line,
        jax.ShapeDtypeStruct((rows, D // BLOCKS), F32),
        line,
        jax.ShapeDtypeStruct((rows, D), F32),
        jax.ShapeDtypeStruct((2 * FF // dp,), F32),
        jax.ShapeDtypeStruct((D // BLOCKS, 2 * FF // dp), F32),
    ) + (line,) * 5

    def specs(arrays):
        by_row = pl.BlockSpec((1, SPAN, D), lambda n: (n, 0, 0))
        return [by_row, by_row] + [
            pl.BlockSpec(v.shape, lambda n, rank=len(v.shape): (0,) * rank) for v in arrays[2:]
        ]

    done = pl.pallas_call(
        functools.partial(finish_kernel, dp),
        grid=(2,),
        out_shape=out_shape,
        in_specs=specs(outs),
        out_specs=specs(out_shape),
        compiler_params=pltpu.CompilerParams(vmem_limit_bytes=63 * 1024 * 1024),
    )(*outs)
    return tuple(done[:9]) + (done[9].T,) + tuple(done[10:])


def solution(mesh):
    rows = P("dp", "blk", None)
    grid = P("dp", "blk")
    line = P("dp")
    in_specs = (rows, P("dp", None)) + (P(),) * 13 + (rows,)
    out_specs = (rows, rows, grid, line, line, grid, line, grid, line, grid) + (line,) * 5
    dp = mesh.shape["dp"]
    return jax.shard_map(
        functools.partial(body, dp),
        mesh=mesh,
        in_specs=in_specs,
        out_specs=out_specs,
        check_vma=False,
    )
```

time: 862 us -> 139 us (0.16); the launches traced: 852 us -> 139 us
  waiting for transfers between devices: 522 us -> 0 us
  Pallas kernels: 0 us -> 138 us
  matrix products: 85.5 us -> 0 us
  local copies, waits for them, and re-layouts: 70.7 us -> 0 us
  other arithmetic: 60.4 us -> 0 us
  blocking collectives: 43.2 us -> 0 us
  starting transfers between devices: 38.9 us -> 0 us
  between operations: 16.5 us -> 0.82 us
  loops' own time: 15.1 us -> 0 us
    reduce_scatter x5 -> x0, waiting for transfers between devices: 474 us -> none  [the longest x1 162 us: body(): lax.psum_scatter(grad_wproj, 'dp', scatter_dimension=0, tiled=True)]
    pallas_call x0 -> x2, Pallas kernels: none -> 138 us  [the longest x1 134 us: body(): pl.pallas_call(functools.partial(kernel, dp, INPUTS + OUTPUTS + tuple(sha...]
    dot_general x18 -> x0, matrix products: 85.5 us -> none  [the longest x1 10.5 us: body(): jnp.einsum('tf,td->fd', hidden_low, grad_top, preferred_element_type=jnp....]
    ppermute x6 -> x0, waiting for transfers between devices: 47.4 us -> none  [shifted(): return lax.ppermute(shard, axis, pairs)]
    ppermute x6 -> x0, starting transfers between devices: 38 us -> none  [shifted(): return lax.ppermute(shard, axis, pairs)]
    unnamed x1 -> x0, blocking collectives: 36.8 us -> none
    unnamed x133 -> x0, local copies, waits for them, and re-layouts: 33.8 us -> none
    convert_element_type x13 -> x0, other arithmetic: 30.1 us -> none  [the longest x2 5.35 us: body(): carried.astype(jnp.bfloat16)]
  transfers between devices with their start and end apart: 14 -> 0, of which waited for: 9 -> 0; matrix products, arithmetic and copies ran while one was open for 17% -> 0% of each run, Pallas kernels for 0% -> 0%
where the time goes in v1:
time: 139 us
  Pallas kernels  138 us (99%)
    pallas_call x1, Pallas kernels, body(): pl.pallas_call(functools.partial(kernel, dp, INPUTS + OUTPUTS + tuple(sha...  134 us
    pallas_call x1, Pallas kernels, body(): pl.pallas_call(functools.partial(finish_kernel, dp), grid=(2,), out_shape...  3.56 us

profile of v1, /device:TPU:0, one launch (start us, length us, event | category | flops | bytes accessed | tf_op | source)
XLA Modules:
  0.0 138.8 jit_solution(6067797674241506723)
XLA Ops:
  0.7 134.4 %shard_map.271 = (bf16[2,256,768]{2,1,0:T(8,128)(2,1)}, bf16[2,256,768]{2,1,0:T(8,128)(2,1)}, bf16[2,3,96,384]{3,2,1,0:T(8,128)(2,1)}, f32[96,384]{1,0:T(8,128)}...) custom-call(bf16[2,256,768]{2,1,0:T(8,128)(2,1)} %refs_0_.1, s32[2,8]{1,0:T(2,128)} %refs_1_.1, ...), custom_call_target="tpu_custom_call" | custom-call | tf_op jit(solution)/shard_map/pallas_call | solution.py:1271
  135.1 3.6 %shard_map.272 = (bf16[2,256,768]{2,1,0:T(8,128)(2,1)}, f32[2,256,768]{2,1,0:T(8,128)}, f32[96,576]{1,0:T(8,128)}, f32[96]{0:T(128)}, f32[96]{0:T(128)}, /*index...) custom-call(bf16[2,256,768]{2,1,0:T(8,128)(2,1)} %get-tuple-element., ...), custom_call_target="tpu_custom_call" | custom-call | tf_op jit(solution)/shard_map/pallas_call | solution.py:1302

commit v2 on v1

--- a/solution.py
+++ b/solution.py
@@ -1,4 +1,5 @@
 import functools
+import itertools
 
 import jax
 import jax.numpy as jnp
@@ -26,7 +27,6 @@
 FF = 1536
 CHUNK = 512
 OWN = 96
-EARLY = 56
 
 PA_ORDER = ("x", "zh", "y")
 PB_ORDER = ("zh", "y", "x")
@@ -34,7 +34,7 @@
 FB_ORDER = ("y", "zl", "x", "zh")
 WO_ORDER = ("y", "zl", "x")
 Q_ORDER = ("x", "zl", "zh")
-Q_CHAINS = ((0, 0, 3), (1, 0, 3), (2, 0, 1), (2, 1, 1), (2, 2, 1))
+Q_CHAINS = ((0, 0, 3), (1, 0, 3), (2, 0, 3))
 
 
 PLACES = (
@@ -45,29 +45,25 @@
     + ["last"]
 )
 STEPS = {
-    "branch": ["pa", "ve"],
-    ("pair", 0, 2): ["ve"],
+    "branch": ["pa"],
+    ("pair", 0, -1): ["ve"],
     ("pair", 1, 2): ["ve"],
     ("pair", 1, 1): ["pb", "fa"],
     ("pair", 1, -1): ["fb", "q0"],
-    ("pair", 2, 3): ["ve"],
-    ("pair", 2, 2): ["pa", "ve"],
+    ("pair", 2, 2): ["pa"],
     ("pair", 2, -1): ["wo", "q1", "q0"],
     ("input", 1): ["fb"],
     "last": (
-        ["q2a", "q2b", "q2c", "q0", "pa", "pa", "vl", "fb", "wo", "pb", "q1", "fa", "vl", "q0", "q0", "wo"]
-        + ["q2a", "q2b", "q2c", "pa", "wo", "q2a", "q2b", "pb", "q2c", "fa", "fb", "q1", "pb", "q1", "pb", "wo"]
-        + ["q1", "fa"]
+        ["q2", "q0", "pa", "pa", "vl", "fb", "wo", "pb", "q1", "fa", "vl", "q0", "q0", "wo", "q2", "pa", "wo"]
+        + ["pb", "fa", "fb", "pb", "q1", "pb", "wo", "fa", "sent", "q2", "q1", "q1"]
     ),
 }
 
 
-def numbered(extras):
+def numbered():
     seen, out = {}, {}
     for place in PLACES:
         names = list(STEPS.get(place, ()))
-        if place == "last":
-            names += ["ve"] * extras
         out[place] = []
         for name in names:
             out[place].append((name, seen.get(name, 0)))
@@ -192,20 +188,24 @@
         gin=vm((2, SPAN, D), BF),
         gres=vm((2, SPAN, D), F32),
         gbr=vm((BLOCKS, SPAN, D), BF),
-        dq_t=vm((128, SPAN), F32),
         dk=vm((SEQ, 128), F32),
         dv=vm((SEQ, 128), F32),
         acc_bfc=vm((1, FF), F32),
         acc_qv=vm((2, 1, HALF), F32),
         acc=vm((6, 1, D), F32),
-        early=vm((6 + extras, EARLY, 128), F32),
-        early_r=vm((5 + extras, EARLY, 128), F32),
-        late=vm((dp, 8, 128), F32),
-        late_r=vm((dp, 8, 128), F32),
-        late_s=vm((8, 128), F32),
-        late_q=vm((3, 8, 128), F32),
-        late_send=pltpu.SemaphoreType.DMA((dp + 3,)),
-        late_recv=pltpu.SemaphoreType.DMA((dp + 3,)),
+    )
+    for name in ("early", "late"):
+        shapes.update(
+            {
+                name: vm((dp, 8, 128), F32),
+                name + "_r": vm((dp, 8, 128), F32),
+                name + "_s": vm((8, 128), F32),
+                name + "_q": vm((3, 8, 128), F32),
+                name + "_send": pltpu.SemaphoreType.DMA((dp + 3,)),
+                name + "_recv": pltpu.SemaphoreType.DMA((dp + 3,)),
+            }
+        )
+    shapes.update(
         local=pltpu.SemaphoreType.DMA((16,)),
         send=pltpu.SemaphoreType.DMA((120,)),
         recv=pltpu.SemaphoreType.DMA((120,)),
@@ -489,10 +489,11 @@
                     at = base(i) + SPAN * j
                     a.probs[head, at : at + SPAN, :] = jnp.exp(scores[j] - top).astype(BF)
 
-        def mix_head(e):
-            head = 2 * p + e
-            feats = pl.ds(mul(head, HEAD), HEAD)
-            for i in range(BLOCKS):
+        @pl.when(p >= 0)
+        def _():
+            for e, i in itertools.product(range(2), range(BLOCKS)):
+                head = 2 * p + e
+                feats = pl.ds(mul(head, HEAD), HEAD)
                 rows = slice(SPAN * i, SPAN * i + SPAN)
                 keys_n = SPAN * (i + 1)
                 out = nn(a.v_t[head, :, :keys_n], a.probs[head, base(i) : base(i) + keys_n, :])
@@ -500,7 +501,6 @@
                 a.linv[head, :, rows] = inverse
                 a.o_t[feats, rows] = (out[:HEAD] * inverse).astype(BF)
 
-        loop(2, mix_head)
         a.mix[c, :, cols] = a.o_t[pl.ds(mul(p, 128), 128), :].T
         mix_copy(p).start()
 
@@ -789,48 +789,78 @@
         )
         return chain, finish
 
-    def vector_chain(buf, came):
-        def stage(n, device):
-            def keep():
-                buf[n + 1] = buf[n] + came[n]
-
-            return [lambda: (buf.at[n], came.at[n])], keep, device
-
-        return Chain([stage(n, device) for n, device in enumerate([to0, to1, to2, to_y, to_core] + extra)])
-
-    ve = vector_chain(a.early, a.early_r)
-
-    def late_copy(src, dst, number, device):
-        return pltpu.make_async_remote_copy(
-            src_ref=src,
-            dst_ref=dst,
-            send_sem=a.late_send.at[number],
-            recv_sem=a.late_recv.at[number],
-            device_id=device,
-            device_id_type=MESH,
-        )
-
-    def late_groups():
-        return [late_copy(a.late.at[to[0]], a.late_r.at[n + 1], n, to) for n, to in enumerate(groups)]
-
-    def late_row():
-        row = (to_core, to_y, to_diagonal)
-        return [late_copy(a.late_s, a.late_q.at[n], dp - 1 + n, to) for n, to in enumerate(row)]
-
-    def late_share():
-        for copy in late_groups():
-            copy.wait_recv()
-        total = a.late[d]
-        for n in range(1, dp):
-            total = total + a.late_r[n]
-        a.late_s[...] = total
-        for copy in late_row():
-            copy.start()
-
-    def late_end():
-        for copy in late_row():
-            copy.wait_recv()
-        a.late_out[...] = a.late_s[...] + a.late_q[0] + a.late_q[1] + a.late_q[2]
+    class Spread:
+        def __init__(self, name, out):
+            self.own, self.came, self.sum, self.row, self.send, self.recv = (
+                r[name + end] for end in ("", "_r", "_s", "_q", "_send", "_recv")
+            )
+            self.out = out
+
+        def copy(self, src, dst, number, device):
+            return pltpu.make_async_remote_copy(
+                src_ref=src,
+                dst_ref=dst,
+                send_sem=self.send.at[number],
+                recv_sem=self.recv.at[number],
+                device_id=device,
+                device_id_type=MESH,
+            )
+
+        def to_groups(self):
+            return [self.copy(self.own.at[to[0]], self.came.at[n + 1], n, to) for n, to in enumerate(groups)]
+
+        def to_row(self):
+            row = (to_core, to_y, to_diagonal)
+            return [self.copy(self.sum, self.row.at[n], dp - 1 + n, to) for n, to in enumerate(row)]
+
+        def start(self, tiles):
+            for e in range(dp):
+                pieces = [
+                    jnp.concatenate([v, jnp.zeros((1, 128 - v.shape[1]), F32)], axis=1) if v.shape[1] < 128 else v
+                    for v in tiles(e)
+                ]
+                pieces += [jnp.zeros((8 - len(pieces), 128), F32)]
+                self.own[e] = jnp.concatenate(pieces, axis=0)
+            for copy in self.to_groups():
+                copy.start()
+
+        def step(self, k):
+            if k == 0:
+                for copy in self.to_groups():
+                    copy.wait_recv()
+                total = self.own[d]
+                for n in range(1, dp):
+                    total = total + self.came[n]
+                self.sum[...] = total
+                for copy in self.to_row():
+                    copy.start()
+            else:
+                for copy in self.to_row():
+                    copy.wait_recv()
+                self.out[...] = self.sum[...] + self.row[0] + self.row[1] + self.row[2]
+
+        def sent(self):
+            for copy in self.to_groups() + self.to_row():
+                copy.wait_send()
+
+    spread = dict(ve=Spread("early", a.early_out), vl=Spread("late", a.late_out))
+    share, share_ff = D // dp, 2 * FF // dp
+
+    def early_tiles(e):
+        rows = [a.acc[n, :, share * e : share * e + share] for n in (0, 1, 4, 5)]
+        at = share_ff * e
+        mine = (c == (at % FF) // D).astype(F32)
+        at = at // FF * D + at % D
+        for n in range(0, share_ff, 128):
+            rows.append(a.acc_bfc[:, at + n : at + min(n + 128, share_ff)] * mine)
+        return rows
+
+    def late_tiles(e):
+        half_dp = dp // 2
+        mine = (c == e // half_dp).astype(F32)
+        at, at_half = share * e, share * (e % half_dp)
+        rows = [a.acc[n, :, at : at + share] for n in (2, 3)]
+        return rows + [a.acc_qv[n, :, at_half : at_half + share] * mine for n in range(2)]
 
     qs = [q_chain(n) for n in range(len(Q_CHAINS))]
 
@@ -838,24 +868,28 @@
         chain.arrive(len(chain.stages) - 1)
         out[...] = keep[...].astype(F32) + land[...].astype(F32)
 
-    chains = dict(pa=pa, pb=pb, fa=fa, fb=fb, wo=wo, ve=ve)
+    chains = dict(pa=pa, pb=pb, fa=fa, fb=fb, wo=wo)
     last_steps = dict(
         pa=lambda: finish(pa, a.gpj_out.at[pl.ds(0, OWN)], r["pa_3"].at[t1], r["pa_4"]),
         pb=lambda: finish(pb, a.gpj_out.at[pl.ds(OWN, OWN)], r["pb_3"].at[t1], r["pb_4"]),
         fa=lambda: finish(fa, a.gfc_out.at[:, pl.ds(0, HALF)], fa_own(), fa_last),
         fb=lambda: finish(fb, a.gfc_out.at[:, pl.ds(HALF, HALF)], fb_own(), fb_last),
         wo=lambda: finish(wo, a.gwo_out, wo_lands[3].at[t2], wo_lands[4]),
-        ve=lambda: (ve.arrive(len(ve.stages) - 1), ve.stages[-1][1]()),
     )
-    for n, name in enumerate(("q0", "q1", "q2a", "q2b", "q2c")):
+    for n, name in enumerate(("q0", "q1", "q2")):
         chains[name], last_steps[name] = qs[n]
-    plan = numbered(len(extra))
-    assert sum(len(todo) for todo in plan.values()) == 2 + sum(len(chain.stages) for chain in chains.values())
+    plan = numbered()
+    assert sum(len(todo) for todo in plan.values()) == 5 + sum(len(chain.stages) for chain in chains.values())
+
+    early_done = [chains[name] for name in ("pa", "pb", "fa", "fb", "wo", "q0")] + list(spread.values())
 
     def steps(place):
         for name, k in plan[place]:
-            if name == "vl":
-                (late_share, late_end)[k]()
+            if name in spread:
+                spread[name].step(k)
+            elif name == "sent":
+                for each in early_done:
+                    each.sent()
             elif k == len(chains[name].stages) - 1:
                 last_steps[name]()
             else:
@@ -953,15 +987,7 @@
                 y_own.start()
 
 
-    def pack(rows, vectors):
-        pieces = [v[:, 128 * i : 128 * i + 128] for v in vectors for i in range(v.shape[1] // 128)]
-        pieces += [jnp.zeros((1, 128), F32)] * (rows - len(pieces))
-        return jnp.concatenate(pieces, axis=0)
-
-    a.early[0] = jnp.zeros((EARLY, 128), F32)
-    a.early[0, :24, :] = pack(24, [a.acc[n] for n in (0, 1, 4, 5)])
-    a.early[0, pl.ds(pl.multiple_of(24 + 16 * c, 8), 16), :] = pack(16, [a.acc_bfc[...]])
-    ve.start(0)
+    spread["ve"].start(early_tiles)
 
     b_copy(0).wait_recv()
     b_copy(1).wait_recv()
@@ -983,7 +1009,10 @@
             scaled = jnp.concatenate(parts, axis=0).astype(BF)
             a.hid[rows, 3 * HALF + 128 * p : 3 * HALF + 128 * p + 128] = scaled.T
 
-    loop(4, branch_block)
+    @pl.when(d >= 0)
+    def _():
+        for t in range(BLOCKS):
+            branch_block(t)
 
     steps("branch")
     for n in range(2):
@@ -1010,50 +1039,66 @@
         cols = pl.ds(mul(p, 128), 128)
         do_cols = pl.ds(pl.multiple_of(3 * HALF + 128 * p, 128), 128)
         a.k_t[...] = a.kn[:, cols].T
-        for i in reversed(range(BLOCKS)):
-            rows = slice(SPAN * i, SPAN * i + SPAN)
-            keys_n = SPAN * (i + 1)
-            pair = a.qn[rows, cols]
-            do_pair = a.hid[rows, do_cols]
-
-            def grad_scores(e):
+        masks = [lane < HEAD, lane >= HEAD]
+
+        def rows_of(i):
+            return slice(SPAN * i, SPAN * i + SPAN)
+
+        def tile(e, i, j):
+            n = i * (i + 1) // 2 + j
+            if e == 0:
+                return a.wproj.at[pl.ds(SPAN * (n % 6), SPAN), pl.ds(SPAN * (n // 6), SPAN)]
+            return a.wfc.at[pl.ds(SPAN * (n % 3), SPAN), pl.ds(SPAN * (n // 3), SPAN)]
+
+        def of_head(ref, i, e, at):
+            both = ref[rows_of(i), at]
+            return jnp.where(masks[e], both, jnp.zeros_like(both))
+
+        @pl.when(p >= 0)
+        def _():
+            for i, e in itertools.product(reversed(range(BLOCKS)), range(2)):
                 head = 2 * p + e
-                mine = (lane >= HEAD * e) & (lane < HEAD * e + HEAD)
-                delta = a.delta[head, :, rows]
-                product = nt(a.vn[:keys_n, cols], jnp.where(mine, do_pair, jnp.zeros_like(do_pair)))
+                delta = a.delta[head, :, rows_of(i)]
+                product = nt(a.vn[: SPAN * (i + 1), cols], of_head(a.hid, i, e, do_cols))
                 for j in range(i + 1):
                     at = base(i) + SPAN * j
-                    keys = slice(SPAN * j, SPAN * j + SPAN)
                     weights = a.probs[head, at : at + SPAN, :].astype(F32)
-                    low = (weights * (product[keys] - delta)).astype(BF)
-                    a.mix[e, keys, :SPAN] = low
-
-            def grad_query(e):
-                low = a.mix[e, :keys_n, :SPAN]
-                feats = pl.ds(mul(e, HEAD), HEAD)
-                a.dq_t[feats, :] = nn(a.k_t[feats, :keys_n], low) * 0.125
-
-            loop(2, grad_scores)
-            loop(2, grad_query)
-            a.hid[rows, cols] = a.dq_t[...].T.astype(BF)
-            masks = [lane < HEAD, lane >= HEAD]
-            query_both = jnp.concatenate([jnp.where(m, pair, jnp.zeros_like(pair)) for m in masks], axis=0)
-            grad_both = jnp.concatenate([jnp.where(m, do_pair, jnp.zeros_like(pair)) for m in masks], axis=0)
-            keys = slice(0, keys_n)
-            at = base(i)
-            scores = jnp.concatenate([a.mix[n, keys, :SPAN] for n in range(2)], axis=1)
-            weights = jnp.concatenate(
-                [a.probs[2 * p, at : at + keys_n, :], a.probs[2 * p + 1, at : at + keys_n, :]], axis=1
-            )
-            part_k = nn(scores, query_both)
-            part_v = nn(weights, grad_both)
-            if i == BLOCKS - 1:
-                a.dk[...] = part_k
-                a.dv[...] = part_v
-            else:
-                a.dk[keys, :] += part_k
-                a.dv[keys, :] += part_v
-            between(p, i)
+                    tile(e, i, j)[...] = (weights * (product[rows_of(j)] - delta)).astype(BF)
+
+        between(p, 3)
+
+        @pl.when(p >= 0)
+        def _():
+            for i in reversed(range(BLOCKS)):
+                parts = []
+                for e in range(2):
+                    scores = jnp.concatenate([tile(e, i, j)[...] for j in range(i + 1)], axis=0)
+                    parts.append(nn(a.k_t[HEAD * e : HEAD * e + HEAD, : SPAN * (i + 1)], scores))
+                a.hid[rows_of(i), cols] = (jnp.concatenate(parts, axis=0) * 0.125).T.astype(BF)
+
+        between(p, 2)
+
+        @pl.when(p >= 0)
+        def _():
+            for i in reversed(range(BLOCKS)):
+                keys = slice(0, SPAN * (i + 1))
+                at = base(i)
+                scores = [
+                    jnp.concatenate([tile(e, i, j)[...] for j in range(i + 1)], axis=0) for e in range(2)
+                ]
+                weights = [a.probs[2 * p + e, at : at + SPAN * (i + 1), :] for e in range(2)]
+                queries = [of_head(a.qn, i, e, cols) for e in range(2)]
+                grads = [of_head(a.hid, i, e, do_cols) for e in range(2)]
+                part_k = nn(jnp.concatenate(scores, axis=1), jnp.concatenate(queries, axis=0))
+                part_v = nn(jnp.concatenate(weights, axis=1), jnp.concatenate(grads, axis=0))
+                if i == BLOCKS - 1:
+                    a.dk[...] = part_k
+                    a.dv[...] = part_v
+                else:
+                    a.dk[keys, :] += part_k
+                    a.dv[keys, :] += part_v
+
+        between(p, 1)
         at_k = pl.ds(pl.multiple_of(HALF + 128 * p, 128), 128)
         at_v = pl.ds(pl.multiple_of(2 * HALF + 128 * p, 128), 128)
         low_k, low_v = a.dk[...].astype(BF), a.dv[...].astype(BF)
@@ -1128,16 +1173,7 @@
         input_pair(g)
         steps(("input", g))
 
-    share, half_dp = D // dp, dp // 2
-    for e in range(dp):
-        mine = (c == e // half_dp).astype(F32)
-        at, at_half = share * e, share * (e % half_dp)
-        rows = [a.acc[2, :, at : at + share], a.acc[3, :, at : at + share]]
-        rows += [a.acc_qv[n, :, at_half : at_half + share] * mine for n in range(2)]
-        tile = jnp.concatenate(rows + [jnp.zeros((4, share), F32)], axis=0)
-        a.late[e] = jnp.concatenate([tile, jnp.zeros((8, 128 - share), F32)], axis=1)
-    for copy in late_groups():
-        copy.start()
+    spread["vl"].start(late_tiles)
     steps("last")
 
     for n, device in enumerate(extra):
@@ -1173,20 +1209,17 @@
         copy.start()
         copy.wait()
         a.gq_out[other] = a.xc_q[...]
-    a.early_out[...] = a.early[5 + len(extra)]
 
     for copy in pending:
         copy.wait_send()
-    for chain in chains.values():
-        chain.sent()
+    for name in ("q1", "q2"):
+        chains[name].sent()
     for s in range(2):
         a_copy(s).wait_send()
     b_copy(0).wait_send()
     b_copy(1).wait_send()
     for copy in (x_far, x_own):
         copy.wait()
-    for copy in late_groups() + late_row():
-        copy.wait_send()
     assert count[0] <= 120
 
 
@@ -1230,24 +1263,14 @@
             out = jnp.where(sub == n, gpj[:, cols_ff * n : cols_ff * n + cols_ff], out)
         gpj_out[...] = out
 
-        def line(vec, first_row, n):
-            return [vec[first_row + i : first_row + i + 1, :] for i in range(n)]
-
-        def put(out, pieces):
-            whole = jnp.concatenate(pieces, axis=1)
-            size = whole.shape[1]
-            n = size // dp
-            turned = pltpu.roll(jnp.broadcast_to(whole, (8, size)), lax.rem(size - d * n, size), 1)
-            out[...] = turned[0, :n]
-
         bq_out[...] = late[2, :rows]
         bv_out[...] = late[3, :rows]
-        put(bo_out, line(early, 0, 6))
-        put(bf_out, line(early, 24, 6) + line(early, 40, 6) + line(early, 30, 6) + line(early, 46, 6))
-        for out, first_row in zip((rest[0], rest[3], rest[4]), (6, 12, 18)):
-            put(out, line(early, first_row, 6))
-        rest[1][...] = late[0, :rows]
-        rest[2][...] = late[1, :rows]
+        bo_out[...] = early[0, :rows]
+        units = 2 * FF // dp
+        pieces = [early[4 + n : 5 + n, : min(128, units - 128 * n)] for n in range(-(-units // 128))]
+        bf_out[...] = jnp.concatenate(pieces, axis=1)[0]
+        for out, v in zip(rest, (early[1], late[0], late[1], early[2], early[3])):
+            out[...] = v[:rows]
 
 
 def body(dp, layer_input, lengths, w_qkv, b_query, b_value, w_out, b_out, w_fc, b_fc, w_proj, b_proj, *more):
@@ -1264,7 +1287,7 @@
         jax.ShapeDtypeStruct((OWN, HALF), F32),
         jax.ShapeDtypeStruct((OWN, D), F32),
         jax.ShapeDtypeStruct((HALF // 2, HALF), F32),
-        jax.ShapeDtypeStruct((EARLY, 128), F32),
+        jax.ShapeDtypeStruct((8, 128), F32),
         jax.ShapeDtypeStruct((8, 128), F32),
     )
     out_specs = [pl.BlockSpec(memory_space=pl.ANY)] * 2 + [pl.BlockSpec(memory_space=pltpu.VMEM)] * 6

time: 139 us -> 134 us (0.964)
  Pallas kernels: 138 us -> 133 us
    pallas_call x1, Pallas kernels: 134 us -> 129 us  [body(): pl.pallas_call(functools.partial(kernel, dp, INPUTS + OUTPUTS + tuple(sha...]
where the time goes in v2:
time: 134 us; the launch traced here: 133 us
  Pallas kernels  133 us (99%)
    pallas_call x1, Pallas kernels, body(): pl.pallas_call(functools.partial(kernel, dp, INPUTS + OUTPUTS + tuple(sha...  129 us
    pallas_call x1, Pallas kernels, body(): pl.pallas_call(functools.partial(finish_kernel, dp), grid=(2,), out_shape...  3.51 us

profile of v2, /device:TPU:0, one launch (start us, length us, event | category | flops | bytes accessed | tf_op | source)
XLA Modules:
  0.0 133.4 jit_solution(8772761107353898707)
XLA Ops:
  0.7 129.1 %shard_map.271 = (bf16[2,256,768]{2,1,0:T(8,128)(2,1)}, bf16[2,256,768]{2,1,0:T(8,128)(2,1)}, bf16[2,3,96,384]{3,2,1,0:T(8,128)(2,1)}, f32[96,384]{1,0:T(8,128)}...) custom-call(bf16[2,256,768]{2,1,0:T(8,128)(2,1)} %refs_0_.1, s32[2,8]{1,0:T(2,128)} %refs_1_.1, ...), custom_call_target="tpu_custom_call" | custom-call | tf_op jit(solution)/shard_map/pallas_call | solution.py:1294
  129.7 3.5 %shard_map.272 = (bf16[2,256,768]{2,1,0:T(8,128)(2,1)}, f32[2,256,768]{2,1,0:T(8,128)}, f32[96,576]{1,0:T(8,128)}, f32[96]{0:T(128)}, f32[96]{0:T(128)}, /*index...) custom-call(bf16[2,256,768]{2,1,0:T(8,128)(2,1)} %get-tuple-element., ...), custom_call_target="tpu_custom_call" | custom-call | tf_op jit(solution)/shard_map/pallas_call | solution.py:1325

commit v3 on v2

--- a/solution.py
+++ b/solution.py
@@ -47,10 +47,9 @@
 STEPS = {
     "branch": ["pa"],
     ("pair", 0, -1): ["ve"],
-    ("pair", 1, 2): ["ve"],
-    ("pair", 1, 1): ["pb", "fa"],
-    ("pair", 1, -1): ["fb", "q0"],
-    ("pair", 2, 2): ["pa"],
+    ("pair", 1, 3): ["ve"],
+    ("pair", 1, -1): ["pb", "fa", "fb", "q0"],
+    ("pair", 2, 3): ["pa"],
     ("pair", 2, -1): ["wo", "q1", "q0"],
     ("input", 1): ["fb"],
     "last": (
@@ -147,6 +146,16 @@
         half = v.shape[0] // 2
         v = jnp.maximum(v[:half], v[half:])
     return v
+
+
+def ahead(items, product):
+    items = list(items)
+    coming = product(*items[0])
+    for n, item in enumerate(items):
+        here = coming
+        if n + 1 < len(items):
+            coming = product(*items[n + 1])
+        yield item, here
 
 
 def base(i):
@@ -463,43 +472,48 @@
 
     def forward_pair(p):
         cols = pl.ds(mul(p, 128), 128)
-        for i in range(BLOCKS):
+        masks = [lane < HEAD, lane >= HEAD]
+
+        def score(i, e):
+            pair = a.qn[SPAN * i : SPAN * i + SPAN, cols]
+            return nt(a.kn[: SPAN * (i + 1), cols], jnp.where(masks[e], pair, jnp.zeros_like(pair)))
+
+        def weigh(i, e):
+            head = 2 * p + e
+            feats = pl.ds(mul(head, HEAD), HEAD)
             rows = slice(SPAN * i, SPAN * i + SPAN)
             keys_n = SPAN * (i + 1)
-            pair = a.qn[rows, cols]
+            out = nn(a.v_t[head, :, :keys_n], a.probs[head, base(i) : base(i) + keys_n, :])
+            inverse = 1.0 / out[HEAD : HEAD + 1]
+            a.linv[head, :, rows] = inverse
+            a.o_t[feats, rows] = (out[:HEAD] * inverse).astype(BF)
+
+        late = []
+        for (i, e), product in ahead(itertools.product(range(BLOCKS), range(2)), score):
+            head = 2 * p + e
             begin = a.start[i]
-            for e in range(2):
-                head = 2 * p + e
-                query = jnp.where(lane // HEAD == e, pair, jnp.zeros_like(pair))
-                scores, tops = [], []
-                product = nt(a.kn[:keys_n, cols], query)
-                for j in range(i + 1):
-                    s = product[SPAN * j : SPAN * j + SPAN]
-                    ok = key_index + SPAN * j >= begin
-                    if j == i:
-                        ok = ok & (key_index <= query_index)
-                    s = jnp.where(ok, s, big_negative)
-                    scores.append(s)
-                    tops.append(top_of(s))
-                top = tops[0]
-                for here in tops[1:]:
-                    top = jnp.maximum(top, here)
-                top = jnp.max(top, axis=0, keepdims=True)
-                for j in range(i + 1):
-                    at = base(i) + SPAN * j
-                    a.probs[head, at : at + SPAN, :] = jnp.exp(scores[j] - top).astype(BF)
-
-        @pl.when(p >= 0)
-        def _():
-            for e, i in itertools.product(range(2), range(BLOCKS)):
-                head = 2 * p + e
-                feats = pl.ds(mul(head, HEAD), HEAD)
-                rows = slice(SPAN * i, SPAN * i + SPAN)
-                keys_n = SPAN * (i + 1)
-                out = nn(a.v_t[head, :, :keys_n], a.probs[head, base(i) : base(i) + keys_n, :])
-                inverse = 1.0 / out[HEAD : HEAD + 1]
-                a.linv[head, :, rows] = inverse
-                a.o_t[feats, rows] = (out[:HEAD] * inverse).astype(BF)
+            scores, tops = [], []
+            for j in range(i + 1):
+                s = product[SPAN * j : SPAN * j + SPAN]
+                ok = key_index + SPAN * j >= begin
+                if j == i:
+                    ok = ok & (key_index <= query_index)
+                s = jnp.where(ok, s, big_negative)
+                scores.append(s)
+                tops.append(top_of(s))
+            top = tops[0]
+            for here in tops[1:]:
+                top = jnp.maximum(top, here)
+            top = jnp.max(top, axis=0, keepdims=True)
+            for j in range(i + 1):
+                at = base(i) + SPAN * j
+                a.probs[head, at : at + SPAN, :] = jnp.exp(scores[j] - top).astype(BF)
+            late.append((i, e))
+            if len(late) > 1:
+                weigh(*late.pop(0))
+
+        for item in late:
+            weigh(*item)
 
         a.mix[c, :, cols] = a.o_t[pl.ds(mul(p, 128), 128), :].T
         mix_copy(p).start()
@@ -544,9 +558,12 @@
         low = (normed * a.gain_two[...] + a.shift_two[...]).astype(BF)
         for k, rows in enumerate(spans):
             a.wqkv[:, rows] = low[SPAN * k : SPAN * k + SPAN].T
-        for f in range(0, FF, CHUNK):
+        def hidden(f):
+            return nn(low, a.wfc[:, f : f + CHUNK])
+
+        for (f,), product in ahead(((f,) for f in range(0, FF, CHUNK)), hidden):
             here = slice(f, f + CHUNK)
-            value, slope = gelu_both(nn(low, a.wfc[:, here]) + a.bfc[:, here])
+            value, slope = gelu_both(product + a.bfc[:, here])
             value = value.astype(BF)
             a.hid[spans[0], here] = value[:SPAN]
             a.hid[spans[1], here] = value[SPAN:]
@@ -1056,10 +1073,13 @@
 
         @pl.when(p >= 0)
         def _():
-            for i, e in itertools.product(reversed(range(BLOCKS)), range(2)):
+            def grad_of(i, e):
+                return nt(a.vn[: SPAN * (i + 1), cols], of_head(a.hid, i, e, do_cols))
+
+            combos = itertools.product(reversed(range(BLOCKS)), range(2))
+            for (i, e), product in ahead(combos, grad_of):
                 head = 2 * p + e
                 delta = a.delta[head, :, rows_of(i)]
-                product = nt(a.vn[: SPAN * (i + 1), cols], of_head(a.hid, i, e, do_cols))
                 for j in range(i + 1):
                     at = base(i) + SPAN * j
                     weights = a.probs[head, at : at + SPAN, :].astype(F32)
@@ -1069,6 +1089,7 @@
 
         @pl.when(p >= 0)
         def _():
+
             for i in reversed(range(BLOCKS)):
                 parts = []
                 for e in range(2):
@@ -1076,10 +1097,6 @@
                     parts.append(nn(a.k_t[HEAD * e : HEAD * e + HEAD, : SPAN * (i + 1)], scores))
                 a.hid[rows_of(i), cols] = (jnp.concatenate(parts, axis=0) * 0.125).T.astype(BF)
 
-        between(p, 2)
-
-        @pl.when(p >= 0)
-        def _():
             for i in reversed(range(BLOCKS)):
                 keys = slice(0, SPAN * (i + 1))
                 at = base(i)
@@ -1098,15 +1115,12 @@
                     a.dk[keys, :] += part_k
                     a.dv[keys, :] += part_v
 
-        between(p, 1)
-        at_k = pl.ds(pl.multiple_of(HALF + 128 * p, 128), 128)
-        at_v = pl.ds(pl.multiple_of(2 * HALF + 128 * p, 128), 128)
-        low_k, low_v = a.dk[...].astype(BF), a.dv[...].astype(BF)
-        a.hid[:, at_k] = low_k
-        a.hid[:, at_v] = low_v
-
-        @pl.when(p >= 0)
-        def _():
+            at_k = pl.ds(pl.multiple_of(HALF + 128 * p, 128), 128)
+            at_v = pl.ds(pl.multiple_of(2 * HALF + 128 * p, 128), 128)
+            low_k, low_v = a.dk[...].astype(BF), a.dv[...].astype(BF)
+            a.hid[:, at_k] = low_k
+            a.hid[:, at_v] = low_v
+
             both = jnp.concatenate([a.hid[:, cols], a.hid[:, at_k], a.hid[:, at_v]], axis=1)
             ones = jnp.ones((16, SEQ), BF)
             grad = nn(jnp.concatenate([a.ain_t[...], ones], axis=0), both)

time: 134 us -> 134 us (level)
  no operation moved by 1% of the time
where the time goes in v3:
time: 134 us
  Pallas kernels  133 us (99%)
    pallas_call x1, Pallas kernels, body(): pl.pallas_call(functools.partial(kernel, dp, INPUTS + OUTPUTS + tuple(sha...  130 us
    pallas_call x1, Pallas kernels, body(): pl.pallas_call(functools.partial(finish_kernel, dp), grid=(2,), out_shape...  3.51 us

profile of v3, /device:TPU:0, one launch (start us, length us, event | category | flops | bytes accessed | tf_op | source)
XLA Modules:
  0.0 133.9 jit_solution(5071598716440779240)
XLA Ops:
  0.7 129.5 %shard_map.271 = (bf16[2,256,768]{2,1,0:T(8,128)(2,1)}, bf16[2,256,768]{2,1,0:T(8,128)(2,1)}, bf16[2,3,96,384]{3,2,1,0:T(8,128)(2,1)}, f32[96,384]{1,0:T(8,128)}...) custom-call(bf16[2,256,768]{2,1,0:T(8,128)(2,1)} %refs_0_.1, s32[2,8]{1,0:T(2,128)} %refs_1_.1, ...), custom_call_target="tpu_custom_call" | custom-call | tf_op jit(solution)/shard_map/pallas_call | solution.py:1308
  130.2 3.5 %shard_map.272 = (bf16[2,256,768]{2,1,0:T(8,128)(2,1)}, f32[2,256,768]{2,1,0:T(8,128)}, f32[96,576]{1,0:T(8,128)}, f32[96]{0:T(128)}, f32[96]{0:T(128)}, /*index...) custom-call(bf16[2,256,768]{2,1,0:T(8,128)(2,1)} %get-tuple-element., ...), custom_call_target="tpu_custom_call" | custom-call | tf_op jit(solution)/shard_map/pallas_call | solution.py:1339
